TPU v7x, 128 devices: a whole 4x4x4 slice. The times are simulated.
128 devices in a mesh: rows: 32 (over x_lo, z, y), cent: 4 (over x_hi, core).
Axes of the slice: x: 4 (x_hi: 2, x_lo: 2; x = x_hi * 2 + x_lo), y: 4, z: 4, core: 2. Of those that a mesh axis runs over, the one named last changes fastest.
Arguments:
- samples: bfloat16 [32768, 512], P('rows'), may hold values from -6 to 6
- weights: float32 [32768], P('rows'), may hold values from 0.2 to 18, as said below
- targets: float32 [16, 32768], P(None, 'rows'), may hold values from -6 to 6
- predictions: float32 [16, 32768], P(None, 'rows'), may hold values from -3 to 3
- centres: bfloat16 [131072, 512], P('rows'), may hold values from -6 to 6
- coefs: float32 [16, 131072], P(None, 'rows'), may hold values from -7 to 7
- block_index: int32 [2, 12288], P(None, 'cent'), may hold values from 0 to 131071, as said below
Outputs:
- new_coefs: float32 [16, 131072], P(None, 'rows')
- new_predictions: float32 [16, 32768], P(None, 'rows')
Inputs may be any that keep to these rules, and one draw needn't show every extreme that they name: Positive sample weights. `block_index`: no pool index appears twice in the whole array. In every step each aligned block of 3072 entries starting at a multiple of 3072 takes exactly 96 indices from each pool shard (index // 4096).
All inputs are finite; a program needn't handle non-finite values.
Results may differ from a plain program's by a relative error of at most 0.008.
Values may be sent and summed in bfloat16 or wider, within the bound.
A program may use at most 64 MiB of HBM per device.

v0:
```python
import math

import jax
import jax.numpy as jnp
from jax import lax
from jax.sharding import PartitionSpec as P

RIDGE = 1.0


def kernel_tile(rows_x, rows_norm, centre_rows, centre_norm, sharpness, offset):
    products = lax.dot_general(
        rows_x, centre_rows, (((1,), (1,)), ((), ())), preferred_element_type=jnp.float32
    )
    exponent = offset + sharpness * (2.0 * products - rows_norm[:, None] - centre_norm[None, :])
    return jnp.exp(exponent).astype(jnp.bfloat16)


def local(samples, weights, targets, predictions, centres, coefs, block_index):
    feature_count = samples.shape[1]
    rows_dev = samples.shape[0]
    pool_dev = centres.shape[0]
    slice_len = block_index.shape[1]
    target_count = targets.shape[0]
    row_devices = lax.axis_size("rows")
    my_row = lax.axis_index("rows")
    sharpness = 1.3 / math.sqrt(8.0 * feature_count)
    offset = 2.0 * feature_count * sharpness - 1.5 - 0.5 * math.log(rows_dev * row_devices)
    block_rows = math.gcd(rows_dev, 512)
    row_norm = jnp.sum(jnp.square(samples.astype(jnp.float32)), axis=1)
    coef_now = coefs
    pred_now = predictions
    for step_idx in range(block_index.shape[0]):
        chosen_idx = block_index[step_idx]
        owners = chosen_idx // pool_dev
        local_pos = chosen_idx - owners * pool_dev
        is_mine = owners == my_row
        masked = jnp.where(is_mine[:, None], centres[local_pos], jnp.zeros((), jnp.bfloat16))
        centre_rows = lax.psum(masked, "rows").astype(jnp.float32).astype(jnp.bfloat16)
        centre_norm = jnp.sum(jnp.square(centre_rows.astype(jnp.float32)), axis=1)
        own_coefs = jnp.where(is_mine[None, :], coef_now[:, local_pos], 0.0)
        weighted = (weights[None, :] * (targets - pred_now)).astype(jnp.bfloat16)
        gradient = -RIDGE * own_coefs
        col_square = jnp.zeros((1, slice_len), jnp.float32)
        for first_row in range(0, rows_dev, block_rows):
            kernel = kernel_tile(
                samples[first_row : first_row + block_rows],
                row_norm[first_row : first_row + block_rows],
                centre_rows,
                centre_norm,
                sharpness,
                offset,
            )
            gradient = gradient + jnp.dot(
                weighted[:, first_row : first_row + block_rows],
                kernel,
                preferred_element_type=jnp.float32,
            )
            kernel_wide = kernel.astype(jnp.float32)
            row_weight = weights[first_row : first_row + block_rows]
            col_square = col_square + jnp.sum(
                row_weight[:, None] * kernel_wide * kernel_wide, axis=0, keepdims=True
            )
        gradient, col_square = lax.psum((gradient, col_square), "rows")
        change_coef = gradient / (col_square + RIDGE)
        coef_low = change_coef.astype(jnp.bfloat16)
        pieces = []
        for first_row in range(0, rows_dev, block_rows):
            kernel = kernel_tile(
                samples[first_row : first_row + block_rows],
                row_norm[first_row : first_row + block_rows],
                centre_rows,
                centre_norm,
                sharpness,
                offset,
            )
            pieces.append(
                lax.dot_general(
                    coef_low, kernel, (((1,), (1,)), ((), ())), preferred_element_type=jnp.float32
                )
            )
        change = jnp.concatenate(pieces, axis=1)
        write_pos = jnp.where(is_mine, local_pos, pool_dev)
        update = (
            jnp.zeros((target_count, pool_dev), jnp.float32)
            .at[:, write_pos]
            .add(change_coef, mode="drop")
        )
        change, update = lax.psum((change, update), "cent")
        coef_now = coef_now + update
        pred_now = pred_now + change
    return (coef_now, pred_now)


def solution(mesh):
    in_specs = (
        P("rows", None),
        P("rows"),
        P(None, "rows"),
        P(None, "rows"),
        P("rows", None),
        P(None, "rows"),
        P(None, "cent"),
    )
    out_specs = (P(None, "rows"), P(None, "rows"))
    return jax.shard_map(local, mesh=mesh, in_specs=in_specs, out_specs=out_specs, check_vma=False)
```

profile of v0, /device:TPU:1, one launch (start us, length us, event | category | flops | bytes accessed | tf_op | source)
XLA Modules:
  0.0 1198.6 jit_solution(9419960183022120283)
XLA Ops:
  7.2 0.8 fusion.34
  8.1 1.4 compare_select_fusion.1
  9.5 0.9 compare_select_fusion.2
  10.4 0.6 copy-done.15
  11.0 16.0 %gather_fusion.3 = bf16[3072,512]{1,0:T(8,128)(2,1)} fusion(bf16[4096,512]{1,0:T(8,128)(2,1)} %param.11, s32[3072]{0:T(1024)S(1)} %broadcast_clamp_fusion), kind=kCustom, calls=%fused_computation.3 | custom fusion | bytes 6303744 | tf_op jit(solution)/shard_map/gather | solution.py:38
  27.0 13.9 %gather_fusion.1 = bf16[3072,512]{1,0:T(8,128)(2,1)S(1)} fusion(bf16[4096,512]{1,0:T(8,128)(2,1)} %param.11, s32[3072]{0:T(1024)S(1)} %broadcast_clamp_fusion.1), kind=kCustom, calls=%fused_computation.1 | custom fusion | bytes 6303744 | tf_op jit(solution)/shard_map/gather | solution.py:38
  41.0 4.1 broadcast_select_fusion
  45.1 2.8 broadcast_select_fusion.1
  48.2 1.6 copy.19
  49.9 10.9 gather_fusion
  60.8 1.8 copy.17
  62.6 0.8 compare_reduce_fusion
  63.7 0.6 fusion.36
  64.3 0.6 fusion.35
  64.9 0.6 compare_select_fusion.3
  65.5 300.2 %all-reduce.18.cloned.1.call-done = (bf16[3072,512]{1,0:T(8,128)(2,1)}, bf16[3072,512]{1,0:T(8,128)(2,1)}) async-done(((bf16[3072,512]{1,0:T(8,128)(2,1)}, bf16[3072,512]{1,0:T(8,128)(2,1)}), (bf16[3072,512]{1,0:T(8,128)(2,1)}, bf16[3072,512]{1,0:T(8,128)(2,1)})) %all-reduce.18.cloned.1.call-update) | async-done | bytes 6291472 | tf_op jit(solution)/shard_map/psum | solution.py:39
  365.7 2.7 multiply_reduce_fusion.1
  368.6 0.7 multiply_reduce_fusion
  369.5 3.6 exponential_convert_fusion.2
  373.2 2.5 exponential_convert_fusion.3
  375.7 5.1 fusion.3
  380.8 5.1 fusion.2
  386.4 1.2 convolution_add_fusion.2
  387.7 130.7 %all-reduce = (f32[1,3072]{1,0:T(1,128)S(1)}, f32[1,3072]{1,0:T(1,128)}) all-reduce(f32[1,3072]{1,0:T(1,128)S(1)} %bitcast.75, f32[1,3072]{1,0:T(1,128)S(1)} %bitcast.74), channel_id=1, replica_groups=mesh['rows'=32,'cent'=4] {'rows'}, use_global_device_ids=true, to_apply=%region_6.7 | all-reduce | flops 6144 | bytes 49152 | tf_op jit(solution)/shard_map/psum | solution.py:64
  518.4 164.3 %all-reduce.10.cloned.1.call-done = f32[16,3072]{1,0:T(8,128)} async-done(((f32[16,3072]{1,0:T(8,128)}), f32[16,3072]{1,0:T(8,128)}) %all-reduce.10.cloned.1.call-update) | async-done | bytes 196624 | tf_op jit(solution)/shard_map/psum | solution.py:64
  682.7 1.0 fusion.13
  683.8 1.6 copy.18
  685.4 2.9 fusion.32
  688.3 0.9 fusion.30
  689.2 0.7 pad_maximum_fusion
  689.9 18.7 %scatter_custom_fusion = f32[16,4096]{0,1:T(8,128)} fusion(s32[3072]{0:T(1024)} %bitcast.79, f32[3072,16]{1,0:T(8,128)} %copy.18, f32[]{:T(128)} %constant.32.clone.1), kind=kCustom, calls=%fused_computation.29 | custom fusion | flops 49152 | bytes 262656 | tf_op jit(solution)/shard_map/scatter-add | solution.py:87
  708.6 78.7 %all-reduce.16.cloned.1.call-done = (f32[16,4096]{0,1:T(8,128)}, f32[16,1024]{1,0:T(8,128)}) async-done(((f32[16,4096]{0,1:T(8,128)}, f32[16,1024]{1,0:T(8,128)}), (f32[16,4096]{0,1:T(8,128)}, f32[16,1024]{1,0:T(8,128)})) %all-reduce.16.cloned.1.call-update) | async-done | bytes 327696 | tf_op jit(solution)/shard_map/psum | solution.py:89
  787.4 2.4 add.181
  789.9 10.8 gather_fusion.2
  800.7 1.8 copy.20
  802.6 2.6 convolution_add_fusion.1
  805.4 1.2 convolution_add_fusion
  806.7 274.0 %all-reduce.12.cloned.1.call-done = f32[16,3072]{1,0:T(8,128)} async-done(((f32[16,3072]{1,0:T(8,128)}), f32[16,3072]{1,0:T(8,128)}) %all-reduce.12.cloned.1.call-update) | async-done | bytes 196624 | tf_op jit(solution)/shard_map/psum | solution.py:64
  1080.7 1.0 fusion.15
  1081.7 1.6 copy.21
  1083.3 3.0 fusion.28
  1086.4 0.9 fusion.26
  1087.3 0.7 pad_maximum_fusion.1
  1088.0 18.7 %scatter_custom_fusion.1 = f32[16,4096]{0,1:T(8,128)} fusion(s32[3072]{0:T(1024)} %bitcast.78, f32[3072,16]{1,0:T(8,128)} %copy.21, f32[]{:T(128)} %constant.32.clone.1), kind=kCustom, calls=%fused_computation.27 | custom fusion | flops 49152 | bytes 262656 | tf_op jit(solution)/shard_map/scatter-add | solution.py:87
  1106.6 78.8 %all-reduce.14.cloned.1.call-done = (f32[16,4096]{0,1:T(8,128)}, f32[16,1024]{1,0:T(8,128)}) async-done(((f32[16,4096]{0,1:T(8,128)}, f32[16,1024]{1,0:T(8,128)}), (f32[16,4096]{0,1:T(8,128)}, f32[16,1024]{1,0:T(8,128)})) %all-reduce.14.cloned.1.call-update) | async-done | bytes 327696 | tf_op jit(solution)/shard_map/psum | solution.py:89
  1185.4 3.2 add.192
  1188.6 2.9 copy.22
  1191.5 0.6 add.193
  (72 shorter events, 2.1 us)
Async XLA Ops:
  7.2 358.6 %all-reduce.18.cloned.1.call-start = ((), (), s32[]{:S(2)}) async-start(), calls=%async_computation.4 | async-start | bytes 12582912 | tf_op jit(solution)/shard_map/psum | solution.py:39
  10.4 0.6 copy-start.15
  47.9 14.7 %copy-start.10 = (s32[2,3072]{1,0:T(2,128)S(1)}, s32[2,3072]{1,0:T(2,128)}, u32[]{:S(2)}) copy-start(s32[2,3072]{1,0:T(2,128)} %param.13) | copy-start | bytes 73732
  48.0 15.4 %copy-start.8 = (bf16[1024,512]{1,0:T(8,128)(2,1)S(1)}, bf16[1024,512]{1,0:T(8,128)(2,1)}, u32[]{:S(2)}) copy-start(bf16[1024,512]{1,0:T(8,128)(2,1)} %param.7) | copy-start | bytes 3145732
  48.0 16.3 %copy-start.19 = (f32[1024]{0:T(1024)S(1)}, f32[1024]{0:T(1024)}, u32[]{:S(2)}) copy-start(f32[1024]{0:T(1024)} %param.8) | copy-start | bytes 12292
  48.0 16.9 %copy-start.11 = (f32[16,1024]{1,0:T(8,128)S(1)}, f32[16,1024]{1,0:T(8,128)}, u32[]{:S(2)}) copy-start(f32[16,1024]{1,0:T(8,128)} %param.9) | copy-start | bytes 196612
  48.0 16.9 %copy-start.13 = (f32[16,1024]{1,0:T(8,128)S(1)}, f32[16,1024]{1,0:T(8,128)}, u32[]{:S(2)}) copy-start(f32[16,1024]{1,0:T(8,128)} %param.10) | copy-start | bytes 196612
  48.0 634.7 %all-reduce.10.cloned.1.call-start = ((), (), s32[]{:S(2)}) async-start(), calls=%async_computation | async-start | bytes 393216 | tf_op jit(solution)/shard_map/psum | solution.py:64
  49.9 318.6 %copy-start = (f32[16,4096]{0,1:T(8,128)}, f32[16,4096]{0,1:T(8,128)S(1)}, u32[]{:S(2)}) copy-start(f32[16,4096]{0,1:T(8,128)S(1)} %copy.19) | copy-start | bytes 786436
  365.7 2.8 copy-start.4
  365.7 3.8 copy-start.5
  365.7 3.8 copy-start.24
  369.5 3.6 copy-start.9
  369.5 3.6 copy-start.22
  373.1 2.5 copy-start.25
  375.6 10.2 copy-start.3
  375.7 5.1 copy-start.23
  387.6 399.7 %all-reduce.16.cloned.1.call-start = ((), (), s32[]{:S(2)}) async-start(), calls=%async_computation.3 | async-start | bytes 4325376 | tf_op jit(solution)/shard_map/psum | solution.py:89
  682.7 5.6 copy-start.6
  708.6 372.1 %all-reduce.12.cloned.1.call-start = ((), (), s32[]{:S(2)}) async-start(), calls=%async_computation.1 | async-start | bytes 393216 | tf_op jit(solution)/shard_map/psum | solution.py:64
  787.4 2.5 copy-start.16
  789.8 12.7 %copy-start.12 = (f32[16,1024]{1,0:T(8,128)S(1)}, f32[16,1024]{1,0:T(8,128)}, u32[]{:S(2)}) copy-start(f32[16,1024]{1,0:T(8,128)} %param.9) | copy-start | bytes 196612
  789.8 12.7 %copy-start.14 = (f32[16,1024]{1,0:T(8,128)S(1)}, f32[16,1024]{1,0:T(8,128)}, u32[]{:S(2)}) copy-start(f32[16,1024]{1,0:T(8,128)} %param.10) | copy-start | bytes 196612
  789.8 12.7 %copy-start.18 = (f32[16,1024]{1,0:T(8,128)S(1)}, f32[16,1024]{1,0:T(8,128)}, u32[]{:S(2)}) copy-start(f32[16,1024]{1,0:T(8,128)} %get-tuple-element.17) | copy-start | bytes 196612
  789.8 12.7 %copy-start.20 = (pred[3072]{0:T(1024)(128)(4,1)S(1)}, pred[3072]{0:T(1024)(128)(4,1)}, u32[]{:S(2)}) copy-start(pred[3072]{0:T(1024)(128)(4,1)} %get-tuple-element.6) | copy-start | bytes 9220
  802.5 2.8 copy-start.1
  802.6 4.1 copy-start.21
  806.6 378.8 %all-reduce.14.cloned.1.call-start = ((), (), s32[]{:S(2)}) async-start(), calls=%async_computation.2 | async-start | bytes 4325376 | tf_op jit(solution)/shard_map/psum | solution.py:89
  1080.7 5.7 copy-start.7
  1083.3 3.1 copy-start.2
  1185.4 6.1 copy-start.17
Sparse Core Ops, SparseCore 0:
  48.1 317.6 all-reduce.17
  387.8 294.9 all-reduce.9
  708.7 78.5 all-reduce.15
  806.7 273.9 all-reduce.11
  1106.8 78.5 all-reduce.13
where the time goes:
time: 1200 us
  waiting for transfers between devices  896 us (75%)
  blocking collectives  131 us (11%)
  local copies, waits for them, and re-layouts  66.3 us (6%)
  other arithmetic  61.4 us (5%)
  matrix products  29.6 us (2%)
  between operations  14.1 us (1%)
    psum x2, waiting for transfers between devices, local(): gradient, col_square = lax.psum((gradient, col_square), 'rows')  438 us
    psum x1, waiting for transfers between devices, local(): lax.psum(masked, 'rows').astype(jnp.float32).astype(jnp.bfloat16)  300 us
    psum x2, waiting for transfers between devices, local(): change, update = lax.psum((change, update), 'cent')  157 us
    psum x1, blocking collectives, local(): gradient, col_square = lax.psum((gradient, col_square), 'rows')  131 us
    scatter-add x2, other arithmetic, local(): update = jnp.zeros((target_count, pool_dev), jnp.float32).at[:, write_pos...  37.3 us
    gather x2, local copies, waits for them, and re-layouts, local(): centres[local_pos]  29.9 us
    gather x4, local copies, waits for them, and re-layouts, local(): own_coefs = jnp.where(is_mine[None, :], coef_now[:, local_pos], 0.0)  25.4 us
  transfers between devices with their start and end apart: 5, of which 5 were waited for; matrix products, arithmetic and copies ran while one was open for 1% of the time, Pallas kernels for 0%

commit v1 on v0

v1 whole, which is shorter than its diff:
```python
import functools
import math

import jax
import jax.numpy as jnp
from jax import lax
from jax.experimental import pallas as pl
from jax.experimental.pallas import tpu as pltpu
from jax.sharding import PartitionSpec as P

RIDGE = 1.0
MESH = pl.DeviceIdType.MESH
F32, BF16 = jnp.float32, jnp.bfloat16
LOG2E = 1.4426950408889634
NT = (((1,), (1,)), ((), ()))


def extract(scale, blk, centres, coefs, samples, weights, targets, preds,
            picked, own_coef, place, weighted, aux, samples_t, select):
    pool = centres.shape[0]
    first = lax.axis_index("rows") * pool
    q_rows = blk.shape[1]
    upper = (lax.broadcasted_iota(jnp.int32, (128, 128), 0)
             <= lax.broadcasted_iota(jnp.int32, (128, 128), 1)).astype(F32)
    lower = (lax.broadcasted_iota(jnp.int32, (q_rows, q_rows), 0)
             > lax.broadcasted_iota(jnp.int32, (q_rows, q_rows), 1)).astype(F32)
    rank_of = lax.broadcasted_iota(jnp.int32, (128, 128), 0).astype(F32)
    coef = coefs[...]
    hi = coef.astype(BF16)
    rest = coef - hi.astype(F32)
    mid = rest.astype(BF16)
    low = (rest - mid.astype(F32)).astype(BF16)
    parts = jnp.concatenate([hi, mid, low], axis=0)
    for s in range(2):
        local = blk[s] - first
        mine = jnp.logical_and(local >= 0, local < pool)
        flag = mine.astype(F32)
        inner = jnp.dot(flag, upper, preferred_element_type=F32)
        before = jnp.sum(jnp.dot(lower, flag, preferred_element_type=F32), axis=1, keepdims=True)
        rank = jnp.where(mine, inner + before - 1.0, -1.0)
        local_f = local.astype(F32)
        acc = jnp.zeros((128, 128), F32)
        for q in range(q_rows):
            acc = acc + jnp.where(rank[q : q + 1, :] == rank_of, local_f[q : q + 1, :], 0.0)
        col = jnp.sum(acc, axis=1, keepdims=True)
        row = jnp.sum(acc.T, axis=0, keepdims=True)
        valid = lax.broadcasted_iota(jnp.int32, (128, 1), 0) < 96
        col = jnp.where(valid, col, -1.0)
        row = jnp.where(lax.broadcasted_iota(jnp.int32, (1, 128), 1) < 96, row, -1.0)
        place[s] = jnp.broadcast_to(row, (8, 128))
        for k in range(0, pool, 512):
            lanes = (lax.broadcasted_iota(jnp.int32, (128, 512), 1) + k).astype(F32)
            select[s * 128 : (s + 1) * 128, k : k + 512] = (col == lanes).astype(F32).astype(BF16)
        three = lax.dot_general(parts, select[s * 128 : (s + 1) * 128, :], NT,
                                preferred_element_type=F32)
        own_coef[s] = three[0:16] + three[16:32] + three[32:48]
    rows = jnp.dot(select[...], centres[...], preferred_element_type=F32).astype(BF16)
    picked[0] = rows[0:96]
    picked[1] = rows[128:224]
    x = samples[...]
    samples_t[...] = x.T
    xf = x.astype(F32)
    sq = xf * xf
    sq_hi = sq.astype(BF16)
    sq_lo = (sq - sq_hi.astype(F32)).astype(BF16)
    ones = jnp.ones((16, x.shape[1]), BF16)
    norm = (lax.dot_general(ones, sq_hi, NT, preferred_element_type=F32)
            + lax.dot_general(ones, sq_lo, NT, preferred_element_type=F32))
    w = weights[...]
    aux[...] = jnp.zeros_like(aux)
    aux[0:1, :] = w
    aux[1:2, :] = -scale * norm[0:1, :]
    weighted[...] = (w * (targets[...] - preds[...])).astype(BF16)


def main_kernel(scale, shift, picked, own_coef, place, weighted, aux, samples_t, targets, preds, coefs,
                pred_out, coef_out,
                cent, peer_t, peer_coef, places, wt, peer_wt, auxes, wcat, kt, gpart, grecv, dlow, dall,
                ppart, precv, wt2, pfin,
                xs, xr, cs, cr, gs, gr, ds_, dr, fs, fr, ps, pr, ws, wr, qs, qr, ls, lr):
    r = lax.axis_index("rows")
    c = lax.axis_index("cent")
    xl = r // 16
    me = lax.rem(r, 16)
    z = me // 4
    y = lax.rem(me, 4)
    e = xl * 4 + c

    def wrap(v):
        return lax.rem(v + 8, 4)

    def plane_dev(j):
        return (xl * 16 + j, c)

    def ring_dev(k):
        return ((k // 4) * 16 + me, lax.rem(k, 4))

    barrier = pltpu.get_barrier_semaphore()

    def greet_plane(k, carry):
        pl.semaphore_signal(barrier, inc=1, device_id=plane_dev(lax.rem(me + k, 16)), device_id_type=MESH)
        return carry

    def greet_ring(k, carry):
        pl.semaphore_signal(barrier, inc=1, device_id=ring_dev(lax.rem(e + k, 8)), device_id_type=MESH)
        return carry

    lax.fori_loop(1, 16, greet_plane, 0)
    lax.fori_loop(1, 8, greet_ring, 0)
    pl.semaphore_wait(barrier, 22)

    def remote(src, dst, ssem, rsem, dev):
        return pltpu.make_async_remote_copy(src_ref=src, dst_ref=dst, send_sem=ssem, recv_sem=rsem,
                                            device_id=dev, device_id_type=MESH)

    partner = ((1 - xl) * 16 + me, c)
    across = ((1 - xl) * 16 + me, lax.rem(c + 2, 4))

    def half_copy(s):
        return remote(picked.at[s, pl.ds(48, 48)], cent.at[s, me, pl.ds(48, 48)], xs.at[s], xr.at[s], partner)

    cut = 224
    depth = samples_t.shape[0]
    x_copies = [
        remote(aux, auxes.at[1], xs.at[2], xr.at[2], partner),
        remote(weighted, peer_wt, xs.at[3], xr.at[3], partner),
        remote(samples_t.at[pl.ds(0, cut)], peer_t.at[pl.ds(0, cut)], xs.at[4], xr.at[4], partner),
        remote(samples_t.at[pl.ds(cut, depth - cut)], peer_t.at[pl.ds(cut, depth - cut)], xs.at[5], xr.at[5],
               across),
        remote(own_coef, peer_coef, xs.at[6], xr.at[6], partner),
    ]
    half_copy(0).start()
    half_copy(1).start()

    counters = [0, 0]

    def slot(part, a, b):
        if part == 0:
            return wrap(z + b) * 4 + wrap(y + a)
        return wrap(z + a) * 4 + wrap(y + b)

    started = [[], []]

    def send(s, part, j, a, b):
        n = counters[s]
        counters[s] += 1
        ref = cent.at[s, j, pl.ds(48 * part, 48)]
        cp = remote(ref, ref, cs.at[s, n], cr.at[s, part, j], plane_dev(slot(part, a, b)))
        cp.start()
        started[s].append(cp)

    def got(s, part, j):
        ref = cent.at[s, j, pl.ds(48 * part, 48)]
        remote(ref, ref, cs.at[s, 0], cr.at[s, part, j], plane_dev(slot(part, 1, 0))).wait_recv()

    def launch(s, part):
        for a, b in ((1, 0), (-1, 0), (0, 1), (0, -1)):
            send(s, part, me, a, b)

    for s in range(2):
        cent[s, me, 0:48] = picked[s, 0:48]
    for s in range(2):
        launch(s, 0)
    for cp in x_copies:
        cp.start()

    def share_place(k, carry):
        to = lax.rem(c + k, 4)
        remote(place, places.at[c], ls.at[k], lr.at[c], (r, to)).start()
        return carry

    lax.fori_loop(1, 4, share_place, 0)
    places[c] = place[...]

    def events(s):
        out = []

        def first(part):
            half_copy(s).wait_recv()
            launch(s, part)

        out.append(lambda: first(1))

        def near(part, sign, fwd):
            j = slot(part, -sign, 0)
            got(s, part, j)
            if fwd:
                send(s, part, j, sign, 0)
            send(s, part, j, 0, 1)
            send(s, part, j, 0, -1)

        def far(part):
            j = slot(part, 2, 0)
            got(s, part, j)
            send(s, part, j, 0, 1)
            send(s, part, j, 0, -1)

        def second(part, d, sign):
            j = slot(part, d, -sign)
            got(s, part, j)
            if (sign == 1) == (d in (0, 3)):
                send(s, part, j, 0, sign)

        def last(part, d):
            got(s, part, slot(part, d, 2))

        for part in (0, 1):
            for sign in (1, -1):
                out.append(functools.partial(near, part, sign, (sign == 1) == (s == part)))
        for d in (0, -1, 1, 2):
            if d == 2:
                out.append(functools.partial(far, 0))
                out.append(functools.partial(far, 1))
            for part in (0, 1):
                for sign in (1, -1):
                    out.append(functools.partial(second, part, d % 4, sign))
        for d in range(4):
            for part in (0, 1):
                out.append(functools.partial(last, part, d))
        return out

    auxes[0] = aux[...]
    wt[:, 0:1024] = weighted[...]
    for s in range(2):
        for j in range(16):
            kt[s, j, 96:128, :] = jnp.zeros((32, 2048), BF16)

    def tiles(s, half, groups):
        src = samples_t if half == 0 else peer_t

        def body(g, carry):
            rows = cent[s, pl.ds(g * 4, 4)].reshape(384, 512)
            wide = rows.astype(F32)
            a = shift - scale * jnp.sum(wide * wide, axis=1, keepdims=True)
            for i in range(4):
                prod = jnp.dot(rows, src[:, i * 256 : (i + 1) * 256], preferred_element_type=F32)
                b = auxes[half, 1:2, i * 256 : (i + 1) * 256]
                val = jnp.exp2(prod * (2.0 * scale) + (a + b)).astype(BF16)
                lo = half * 1024 + i * 256
                for q in range(4):
                    kt[s, g * 4 + q, 0:96, lo : lo + 256] = val[q * 96 : (q + 1) * 96]
            return carry

        lax.fori_loop(groups[0], groups[1], body, 0)

    def squares(s, pairs):
        def body(j2, carry):
            k = kt[s, pl.ds(j2 * 2, 2)].reshape(256, 2048)
            sq = lax.dot_general(wcat[...], k * k, NT, preferred_element_type=F32)
            tot = jnp.broadcast_to(sq[0:1] + sq[1:2], (8, 256))
            gpart[s, j2 * 2, 16:24] = tot[:, 0:128]
            gpart[s, j2 * 2 + 1, 16:24] = tot[:, 128:256]
            return carry

        lax.fori_loop(pairs[0], pairs[1], body, 0)

    def g_copy(s, j):
        return remote(gpart.at[s, j], grecv.at[s, me], gs.at[s, j], gr.at[s, me], plane_dev(j))

    def gradient(s, rhs):
        def pair(j2):
            k = kt[s, pl.ds(j2 * 2, 2)].reshape(256, 2048)
            g = lax.dot_general(rhs, k, NT, preferred_element_type=F32)
            gpart[s, j2 * 2, 0:16] = g[:, 0:128]
            gpart[s, j2 * 2 + 1, 0:16] = g[:, 128:256]

        def body(k, carry):
            j2 = lax.rem(me // 2 + k, 8)
            pair(j2)
            g_copy(s, j2 * 2).start()
            g_copy(s, j2 * 2 + 1).start()
            return carry

        lax.fori_loop(1, 8, body, 0)
        pair(me // 2)
        g_copy(s, me + 1 - 2 * lax.rem(me, 2)).start()

    def d_copy(s, j):
        return remote(dlow.at[s, me], dlow.at[s, me], ds_.at[s, j], dr.at[s, me], plane_dev(j))

    def f_copy(s, k):
        return remote(dall.at[s, e], dall.at[s, e], fs.at[s, k], fr.at[s, e], ring_dev(k))

    def make_delta(s):
        total = gpart[s, me]

        def body(k, total):
            j = lax.rem(me + k, 16)
            remote(gpart.at[s, j], grecv.at[s, j], gs.at[s, j], gr.at[s, j], plane_dev(j)).wait_recv()
            return total + grecv[s, j]

        total = lax.fori_loop(1, 16, body, total)
        lane = lax.broadcasted_iota(jnp.int32, (16, 128), 1)
        coef = jnp.where(lane < 48, own_coef[s], peer_coef[s])
        delta = (total[0:16] - RIDGE * coef) / (total[16:17] + RIDGE)
        dlow[s, me] = delta.astype(BF16)
        dall[s, e] = delta

        def push(k, carry):
            d_copy(s, lax.rem(me + k, 16)).start()
            return carry

        lax.fori_loop(1, 16, push, 0)

        def push_ring(k, carry):
            f_copy(s, lax.rem(e + k, 8)).start()
            return carry

        lax.fori_loop(1, 8, push_ring, 0)

    def wait_delta(s):
        def body(k, carry):
            j = lax.rem(me + k, 16)
            remote(dlow.at[s, j], dlow.at[s, j], ds_.at[s, j], dr.at[s, j], plane_dev(j)).wait_recv()
            return carry

        lax.fori_loop(1, 16, body, 0)

    def p_copy(s, to):
        return remote(ppart.at[s, to], precv.at[s, e], ps.at[s, to], pr.at[s, e], ring_dev(to))

    def change(s):
        d = jnp.concatenate([dlow[s, j] for j in range(16)], axis=1)

        def chunk(to):
            rel = lax.rem(to // 4 + xl, 2) * 4 + lax.rem(to, 4)
            k = kt[s, :, :, pl.ds(pl.multiple_of(rel * 256, 256), 256)].reshape(2048, 256)
            ppart[s, to] = jnp.dot(d, k, preferred_element_type=F32)

        def body(k, carry):
            to = lax.rem(e + k, 8)
            chunk(to)
            p_copy(s, to).start()
            return carry

        lax.fori_loop(1, 8, body, 0)
        chunk(e)

    def sum_change(s):
        def body(k, total):
            j = lax.rem(e + k, 8)
            remote(ppart.at[s, j], precv.at[s, j], ps.at[s, j], pr.at[s, j], ring_dev(j)).wait_recv()
            return total + precv[s, j]

        return lax.fori_loop(1, 8, body, ppart[s, e])

    def update_coefs(s, base):
        def body(k, carry):
            j = lax.rem(e + k, 8)
            remote(dall.at[s, j], dall.at[s, j], fs.at[s, j], fr.at[s, j], ring_dev(j)).wait_recv()
            return carry

        lax.fori_loop(1, 8, body, 0)
        lane = lax.broadcasted_iota(jnp.int32, (16, 128), 1)
        pieces, cols = [], []
        for k in range(4):
            own = dall[s, xl * 4 + k]
            other = dall[s, (1 - xl) * 4 + k]
            pieces.append(jnp.where(lane < 48, own, other))
            row = places[k, s, 0:1]
            cols.append(jnp.broadcast_to(row, (128, 128)).T)
        d = jnp.concatenate(pieces, axis=1)
        hi = d.astype(BF16)
        rest = d - hi.astype(F32)
        mid = rest.astype(BF16)
        low = (rest - mid.astype(F32)).astype(BF16)
        lhs = jnp.concatenate([hi, mid, low], axis=0)
        col = jnp.concatenate(cols, axis=0)

        def step(k, carry):
            at = pl.ds(pl.multiple_of(k * 512, 512), 512)
            base_lane = (k * 512).astype(F32)
            hot = []
            for i in range(4):
                lanes = lax.broadcasted_iota(jnp.int32, (512, 128), 1).astype(F32) + (base_lane + i * 128.0)
                hot.append((col == lanes).astype(F32).astype(BF16))
            three = jnp.dot(lhs, jnp.concatenate(hot, axis=1), preferred_element_type=F32)
            coef_out[:, at] = base[:, at] + (three[0:16] + three[16:32] + three[32:48])
            return carry

        lax.fori_loop(0, 8, step, 0)

    for ev in events(0):
        ev()
    x_copies[0].wait_recv()
    w2 = jnp.concatenate([auxes[0, 0:1], auxes[1, 0:1]], axis=1)
    w_hi = w2.astype(BF16).astype(F32)
    row_id = lax.broadcasted_iota(jnp.int32, (16, 2048), 0)
    wcat[...] = jnp.where(row_id == 0, w_hi, jnp.where(row_id == 1, w2 - w_hi, 0.0)).astype(BF16)
    later = events(1)
    cuts = [0, 7, 14, 21, len(later)]
    tiles(0, 0, (0, 2))
    for ev in later[: cuts[1]]:
        ev()
    tiles(0, 0, (2, 4))
    for ev in later[cuts[1] : cuts[2]]:
        ev()
    x_copies[2].wait_recv()
    x_copies[3].wait_recv()
    tiles(0, 1, (0, 2))
    for ev in later[cuts[2] : cuts[3]]:
        ev()
    tiles(0, 1, (2, 4))
    squares(0, (0, 8))
    x_copies[1].wait_recv()
    x_copies[4].wait_recv()
    wt[:, 1024:2048] = peer_wt[...]
    gradient(0, wt[...])
    for ev in later[cuts[3] :]:
        ev()
    tiles(1, 0, (0, 4))
    make_delta(0)
    tiles(1, 1, (0, 4))
    wait_delta(0)
    change(0)
    squares(1, (0, 8))

    def wait_place(k, carry):
        j = lax.rem(c + k, 4)
        remote(place, places.at[j], ls.at[k], lr.at[j], (r, j)).wait_recv()
        return carry

    lax.fori_loop(1, 4, wait_place, 0)
    chunk_at = pl.ds(pl.multiple_of(c * 256, 256), 256)
    pred = preds[:, chunk_at] + sum_change(0)

    def rel_to(to):
        return lax.rem(to // 4 + xl, 2) * 4 + c

    def w_copy(to):
        return remote(wt2.at[c], wt2.at[rel_to(to)], ws.at[to], wr.at[rel_to(to)], ring_dev(to))

    wt2[c] = (auxes[0, 0:1, chunk_at] * (targets[:, chunk_at] - pred)).astype(BF16)

    def push_w(k, carry):
        w_copy(lax.rem(e + k, 8)).start()
        return carry

    lax.fori_loop(1, 8, push_w, 0)
    update_coefs(0, coefs)

    def wait_w(k, carry):
        j = lax.rem(c + k, 8)
        remote(wt2.at[j], wt2.at[j], ws.at[j], wr.at[j], ring_dev(j)).wait_recv()
        return carry

    lax.fori_loop(1, 8, wait_w, 0)
    gradient(1, jnp.concatenate([wt2[j] for j in range(8)], axis=1))
    make_delta(1)
    wait_delta(1)
    change(1)
    update_coefs(1, coef_out)
    pfin[c] = pred + sum_change(1)

    def q_copy(k):
        to = lax.rem(c + k, 4)
        return remote(pfin.at[c], pfin.at[c], qs.at[to], qr.at[c], (r, to))

    def push_q(k, carry):
        q_copy(k).start()
        return carry

    def wait_q(k, carry):
        j = lax.rem(c + k, 4)
        remote(pfin.at[j], pfin.at[j], qs.at[j], qr.at[j], (r, j)).wait_recv()
        return carry

    lax.fori_loop(1, 4, push_q, 0)
    lax.fori_loop(1, 4, wait_q, 0)
    for k in range(4):
        pred_out[:, k * 256 : (k + 1) * 256] = pfin[k]

    for s in range(2):
        half_copy(s).wait_send()
        for cp in started[s]:
            cp.wait_send()
    for cp in x_copies:
        cp.wait_send()

    def drain_plane(k, carry):
        j = lax.rem(me + k, 16)
        for s in range(2):
            g_copy(s, j).wait_send()
            d_copy(s, j).wait_send()
        return carry

    def drain_ring(k, carry):
        j = lax.rem(e + k, 8)
        for s in range(2):
            f_copy(s, j).wait_send()
            p_copy(s, j).wait_send()
        w_copy(j).wait_send()
        return carry

    def drain_cent(k, carry):
        q_copy(k).wait_send()
        remote(place, places.at[c], ls.at[k], lr.at[c], (r, lax.rem(c + k, 4))).wait_send()
        return carry

    lax.fori_loop(1, 16, drain_plane, 0)
    lax.fori_loop(1, 8, drain_ring, 0)
    lax.fori_loop(1, 4, drain_cent, 0)


def local(samples, weights, targets, predictions, centres, coefs, block_index):
    rows, depth = samples.shape
    pool = centres.shape[0]
    t = targets.shape[0]
    sharpness = 1.3 / math.sqrt(8.0 * depth)
    offset = 2.0 * depth * sharpness - 1.5 - 0.5 * math.log(rows * lax.axis_size("rows"))
    scale = sharpness * LOG2E
    shift = offset * LOG2E
    vmem = pl.BlockSpec(memory_space=pltpu.VMEM)
    sds = jax.ShapeDtypeStruct
    prepared = pl.pallas_call(
        functools.partial(extract, scale),
        out_shape=(
            sds((2, 96, depth), BF16),
            sds((2, t, 128), F32),
            sds((2, 8, 128), F32),
            sds((t, rows), BF16),
            sds((8, rows), F32),
            sds((depth, rows), BF16),
        ),
        in_specs=[vmem] * 7,
        out_specs=(vmem,) * 6,
        scratch_shapes=[pltpu.VMEM((256, pool), BF16)],
        compiler_params=pltpu.CompilerParams(vmem_limit_bytes=40 * 2**20),
    )(block_index.reshape(2, -1, 128), centres, coefs, samples, weights[None, :], targets, predictions)
    dma = pltpu.SemaphoreType.DMA
    pred, coef = pl.pallas_call(
        functools.partial(main_kernel, scale, shift),
        out_shape=(sds((t, rows), F32), sds((t, pool), F32)),
        in_specs=[vmem] * 9,
        out_specs=(vmem,) * 2,
        scratch_shapes=[
            pltpu.VMEM((2, 16, 96, depth), BF16),
            pltpu.VMEM((depth, rows), BF16),
            pltpu.VMEM((2, t, 128), F32),
            pltpu.VMEM((4, 2, 8, 128), F32),
            pltpu.VMEM((t, 2 * rows), BF16),
            pltpu.VMEM((t, rows), BF16),
            pltpu.VMEM((2, 8, rows), F32),
            pltpu.VMEM((16, 2 * rows), BF16),
            pltpu.VMEM((2, 16, 128, 2 * rows), BF16),
            pltpu.VMEM((2, 16, 24, 128), F32),
            pltpu.VMEM((2, 16, 24, 128), F32),
            pltpu.VMEM((2, 16, t, 128), BF16),
            pltpu.VMEM((2, 8, t, 128), F32),
            pltpu.VMEM((2, 8, t, 256), F32),
            pltpu.VMEM((2, 8, t, 256), F32),
            pltpu.VMEM((8, t, 256), BF16),
            pltpu.VMEM((4, t, 256), F32),
            dma((7,)), dma((7,)),
            dma((2, 30)), dma((2, 2, 16)),
            dma((2, 16)), dma((2, 16)),
            dma((2, 16)), dma((2, 16)),
            dma((2, 8)), dma((2, 8)),
            dma((2, 8)), dma((2, 8)),
            dma((8,)), dma((8,)),
            dma((4,)), dma((4,)),
            dma((4,)), dma((4,)),
        ],
        compiler_params=pltpu.CompilerParams(
            collective_id=0, has_side_effects=True, vmem_limit_bytes=48 * 2**20
        ),
    )(*prepared, targets, predictions, coefs)
    return coef, pred


def solution(mesh):
    in_specs = (
        P("rows", None),
        P("rows"),
        P(None, "rows"),
        P(None, "rows"),
        P("rows", None),
        P(None, "rows"),
        P(None, "cent"),
    )
    out_specs = (P(None, "rows"), P(None, "rows"))
    return jax.shard_map(local, mesh=mesh, in_specs=in_specs, out_specs=out_specs, check_vma=False)
```

time: 1200 us -> 106 us (0.09)
  waiting for transfers between devices: 896 us -> 0 us
  blocking collectives: 131 us -> 0 us
  Pallas kernels: 0 us -> 96.3 us
  other arithmetic: 61.4 us -> 0 us
  local copies, waits for them, and re-layouts: 66.3 us -> 8.81 us
  matrix products: 29.6 us -> 0 us
  between operations: 14.1 us -> 0.67 us
    psum x5 -> x0, waiting for transfers between devices: 896 us -> none  [the longest x2 438 us: local(): gradient, col_square = lax.psum((gradient, col_square), 'rows')]
    psum x1 -> x0, blocking collectives: 131 us -> none  [local(): gradient, col_square = lax.psum((gradient, col_square), 'rows')]
    pallas_call x0 -> x2, Pallas kernels: none -> 96.3 us  [the longest x1 93.5 us: local(): pl.pallas_call(functools.partial(main_kernel, scale, shift), out_shape=(s...]
    gather x6 -> x0, local copies, waits for them, and re-layouts: 55.3 us -> none  [the longest x2 29.9 us: local(): centres[local_pos]]
    scatter-add x2 -> x0, other arithmetic: 37.3 us -> none  [local(): update = jnp.zeros((target_count, pool_dev), jnp.float32).at[:, write_pos...]
    dot_general x12 -> x0, matrix products: 29.6 us -> none  [the longest x4 16.3 us: kernel_tile(): lax.dot_general(rows_x, centre_rows, (((1,), (1,)), ((), ())), preferred_...]
  transfers between devices with their start and end apart: 5 -> 0, of which waited for: 5 -> 0; matrix products, arithmetic and copies ran while one was open for 1% -> 0% of each run, Pallas kernels for 0% -> 0%
where the time goes in v1:
time: 106 us
  Pallas kernels  96.3 us (91%)
  local copies, waits for them, and re-layouts  8.81 us (8%)
    pallas_call x1, Pallas kernels, local(): pl.pallas_call(functools.partial(main_kernel, scale, shift), out_shape=(s...  93.5 us
    unnamed x21, local copies, waits for them, and re-layouts  8.81 us
    pallas_call x1, Pallas kernels, local(): pl.pallas_call(functools.partial(extract, scale), out_shape=(sds((2, 96,...  2.85 us

profile of v1, /device:TPU:1, one launch (start us, length us, event | category | flops | bytes accessed | tf_op | source)
XLA Modules:
  0.0 105.8 jit_solution(109189551673109786)
XLA Ops:
  0.6 0.7 copy.11
  1.4 0.0 copy-start
  1.4 2.2 %copy-done = bf16[4096,512]{1,0:T(8,128)(2,1)S(1)} copy-done((bf16[4096,512]{1,0:T(8,128)(2,1)S(1)}, bf16[4096,512]{1,0:T(8,128)(2,1)}, u32[]{:S(2)}) %copy-start) | copy-done | bytes 4194328
  3.6 0.0 copy-start.1
  3.6 1.2 %copy-done.1 = bf16[1024,512]{1,0:T(8,128)(2,1)S(1)} copy-done((bf16[1024,512]{1,0:T(8,128)(2,1)S(1)}, bf16[1024,512]{1,0:T(8,128)(2,1)}, u32[]{:S(2)}) %copy-start.1) | copy-done | bytes 1048600
  4.8 0.0 copy-start.2
  4.8 0.9 copy-done.2
  5.7 0.0 copy-start.4
  5.7 0.8 copy-done.4
  6.6 0.0 copy-start.6
  6.6 0.8 copy-done.6
  7.4 0.0 copy-start.8
  7.4 0.7 copy-done.8
  8.1 0.0 copy-start.3
  8.1 0.0 copy-start.5
  8.1 0.0 copy-start.7
  8.1 2.9 %shard_map.86 = (bf16[2,96,512]{2,1,0:T(8,128)(2,1)S(1)}, f32[2,16,128]{2,1,0:T(8,128)S(1)}, f32[2,8,128]{2,1,0:T(8,128)S(1)}, bf16[16,1024]{1,0:T(8,128)(2,1)S(...) custom-call(s32[2,24,128]{2,1,0:T(8,128)S(1)} %bitcast.5, bf16[4096,512]{1,0:T(8,128)(2,1)S(1)} %copy-done, ...), custom_call_target="tpu_custom_call" | custom-call | tf_op jit(solution)/shard_map/pallas_call | solution.py:515
  11.0 0.0 copy-done.3
  11.0 0.0 copy-done.5
  11.0 0.0 copy-done.7
  11.0 93.5 %shard_map.87 = (f32[16,1024]{1,0:T(8,128)S(1)}, f32[16,4096]{1,0:T(8,128)S(1)}) custom-call(bf16[2,96,512]{2,1,0:T(8,128)(2,1)S(1)} %get-tuple-element.10.picked, f32[2,16,128]{2,1,0:T(8,128)S(1)} %get-tuple-element.11.own_coef, f32[2,8,128]{2,1,0:T(8,128)S(1)} %get-tuple-element.12.place, bf16[16,1024]{1,0:T(8,128)(2,1)S(1)} %get-tuple-element.13.weighted, ...), custom_call_target="tpu_custom_call" | custom-call | tf_op jit(solution)/shard_map/pallas_call | solution.py:531
  104.5 0.7 copy.14
  105.2 0.6 copy.15
Async XLA Ops:
  1.4 2.2 %copy-start = (bf16[4096,512]{1,0:T(8,128)(2,1)S(1)}, bf16[4096,512]{1,0:T(8,128)(2,1)}, u32[]{:S(2)}) copy-start(bf16[4096,512]{1,0:T(8,128)(2,1)} %centres.1) | copy-start | bytes 12582916
  3.6 1.2 %copy-start.1 = (bf16[1024,512]{1,0:T(8,128)(2,1)S(1)}, bf16[1024,512]{1,0:T(8,128)(2,1)}, u32[]{:S(2)}) copy-start(bf16[1024,512]{1,0:T(8,128)(2,1)} %samples.1) | copy-start | bytes 3145732
  4.8 0.9 copy-start.2
  5.7 0.8 copy-start.4
  6.6 0.8 copy-start.6
  7.4 0.7 copy-start.8
  8.1 2.9 %copy-start.3 = (f32[16,4096]{1,0:T(8,128)S(1)}, f32[16,4096]{1,0:T(8,128)}, u32[]{:S(2)}) copy-start(f32[16,4096]{1,0:T(8,128)} %coefs.3) | copy-start | bytes 786436
  8.1 2.9 %copy-start.5 = (f32[16,1024]{1,0:T(8,128)S(1)}, f32[16,1024]{1,0:T(8,128)}, u32[]{:S(2)}) copy-start(f32[16,1024]{1,0:T(8,128)} %targets.3) | copy-start | bytes 196612
  8.1 2.9 %copy-start.7 = (f32[16,1024]{1,0:T(8,128)S(1)}, f32[16,1024]{1,0:T(8,128)}, u32[]{:S(2)}) copy-start(f32[16,1024]{1,0:T(8,128)} %preds.3) | copy-start | bytes 196612

commit v2 on v1

v2 whole, which is shorter than its diff:
```python
import functools
import math

import jax
import jax.numpy as jnp
from jax import lax
from jax.experimental import pallas as pl
from jax.experimental.pallas import tpu as pltpu
from jax.sharding import PartitionSpec as P

RIDGE = 1.0
MESH = pl.DeviceIdType.MESH
F32, BF16 = jnp.float32, jnp.bfloat16
LOG2E = 1.4426950408889634
NT = (((1,), (1,)), ((), ()))


def iota(shape, axis):
    return lax.broadcasted_iota(jnp.int32, shape, axis)


def split3(v):
    hi = v.astype(BF16)
    rest = v - hi.astype(F32)
    mid = rest.astype(BF16)
    low = (rest - mid.astype(F32)).astype(BF16)
    return jnp.concatenate([hi, mid, low], axis=0)


def sum3(v):
    return v[0:16] + v[16:32] + v[32:48]


def main_kernel(scale, shift, blk_in, centres_in, coefs_in, samples_in, weights_in, targets_in, preds_in,
                pred_out, coef_out,
                blk, centres, coefs, samples, weights, targets, preds, select,
                outgoing, own_coef, place, weighted, samples_t,
                cent, peer_t, peer_coef, places, wt, peer_wt, auxes, wcat, kt, gsend, grecv, sqsend, sqrecv,
                dlow, dall, psend, precv, lsend, lrecv, wt2, pmid, pend,
                loads, xs, xr, cs, cr, gs, gr, ss, sr, ds_, dr, fs, fr, ps, pr, es, er, ws, wr, qs, qr, ls, lr,
                hs, hr):
    r = lax.axis_index("rows")
    c = lax.axis_index("cent")
    xl = r // 16
    me = lax.rem(r, 16)
    z = me // 4
    y = lax.rem(me, 4)
    e = xl * 4 + c
    core = lax.rem(c, 2)

    def wrap(v):
        return lax.rem(v + 8, 4)

    def plane_dev(j):
        return (xl * 16 + j, c)

    def ring_dev(k):
        return ((k // 4) * 16 + me, lax.rem(k, 4))

    pairs = ((blk_in, blk), (centres_in, centres), (samples_in, samples), (coefs_in, coefs),
             (weights_in, weights), (targets_in, targets), (preds_in, preds))
    fetch = [pltpu.make_async_copy(src, dst, loads.at[i]) for i, (src, dst) in enumerate(pairs)]
    for cp in fetch:
        cp.start()

    barrier = pltpu.get_barrier_semaphore()

    def greet_plane(k, carry):
        pl.semaphore_signal(barrier, inc=1, device_id=plane_dev(lax.rem(me + k, 16)), device_id_type=MESH)
        return carry

    def greet_ring(k, carry):
        pl.semaphore_signal(barrier, inc=1, device_id=ring_dev(lax.rem(e + k, 8)), device_id_type=MESH)
        return carry

    lax.fori_loop(1, 16, greet_plane, 0)
    lax.fori_loop(1, 8, greet_ring, 0)

    pool = centres.shape[0]
    q_rows = blk.shape[1] // 128
    upper = (iota((128, 128), 0) <= iota((128, 128), 1)).astype(F32)
    lower = (iota((q_rows, q_rows), 0) > iota((q_rows, q_rows), 1)).astype(F32)
    rank_of = iota((128, 128), 0).astype(F32)
    fetch[0].wait()
    for s in range(2):
        index = jnp.concatenate([blk[s : s + 1, q * 128 : (q + 1) * 128] for q in range(q_rows)], axis=0)
        at = index - r * pool
        mine = jnp.logical_and(at >= 0, at < pool)
        flag = mine.astype(F32)
        inner = jnp.dot(flag, upper, preferred_element_type=F32)
        before = jnp.sum(jnp.dot(lower, flag, preferred_element_type=F32), axis=1, keepdims=True)
        rank = jnp.where(mine, inner + before - 1.0, -1.0)
        at_f = at.astype(F32)
        acc = jnp.zeros((128, 128), F32)
        for q in range(q_rows):
            acc = acc + jnp.where(rank[q : q + 1, :] == rank_of, at_f[q : q + 1, :], 0.0)
        col = jnp.where(iota((128, 1), 0) < 96, jnp.sum(acc, axis=1, keepdims=True), -1.0)
        row = jnp.where(iota((1, 128), 1) < 96, jnp.sum(acc.T, axis=0, keepdims=True), -1.0)
        place[s] = jnp.broadcast_to(row, (8, 128))
        for k in range(0, pool, 512):
            lanes = (iota((128, 512), 1) + k).astype(F32)
            select[s * 128 : (s + 1) * 128, k : k + 512] = (col == lanes).astype(F32).astype(BF16)
    fetch[1].wait()
    rows = jnp.dot(select[...], centres[...], preferred_element_type=F32).astype(BF16)
    for s in range(2):
        cent[s, me, 0:48] = rows[s * 128 : s * 128 + 48]
        outgoing[s] = rows[s * 128 + 48 : s * 128 + 96]
    fetch[2].wait()
    samples_t[...] = samples[...].T

    pl.semaphore_wait(barrier, 22)

    def remote(src, dst, ssem, rsem, dev):
        return pltpu.make_async_remote_copy(src_ref=src, dst_ref=dst, send_sem=ssem, recv_sem=rsem,
                                            device_id=dev, device_id_type=MESH)

    partner = ((1 - xl) * 16 + me, c)
    across = ((1 - xl) * 16 + me, lax.rem(c + 2, 4))
    sibling = (r, c + 1 - 2 * core)

    def half_copy(s):
        return remote(outgoing.at[s], cent.at[s, me, pl.ds(48, 48)], xs.at[s], xr.at[s], partner)

    counters = [0, 0]
    started = [[], []]

    def slot(part, a, b):
        if part == 0:
            return wrap(z + b) * 4 + wrap(y + a)
        return wrap(z + a) * 4 + wrap(y + b)

    def send(s, part, j, a, b):
        n = counters[s]
        counters[s] += 1
        ref = cent.at[s, j, pl.ds(48 * part, 48)]
        cp = remote(ref, ref, cs.at[s, n], cr.at[s, part, j], plane_dev(slot(part, a, b)))
        cp.start()
        started[s].append(cp)

    def got(s, part, j):
        ref = cent.at[s, j, pl.ds(48 * part, 48)]
        remote(ref, ref, cs.at[s, 0], cr.at[s, part, j], plane_dev(slot(part, 1, 0))).wait_recv()

    def launch(s, part):
        for a, b in ((1, 0), (-1, 0), (0, 1), (0, -1)):
            send(s, part, me, a, b)

    def near(s, part, sign):
        j = slot(part, -sign, 0)
        got(s, part, j)
        if (sign == 1) == (s == part):
            send(s, part, j, sign, 0)
        send(s, part, j, 0, 1)
        send(s, part, j, 0, -1)

    def far(s, part):
        j = slot(part, 2, 0)
        got(s, part, j)
        send(s, part, j, 0, 1)
        send(s, part, j, 0, -1)

    def second(s, part, d, sign):
        j = slot(part, d, -sign)
        got(s, part, j)
        if (sign == 1) == (d in (0, -1)):
            send(s, part, j, 0, sign)

    def last(s, part, d):
        got(s, part, slot(part, d, 2))

    def level(s, n):
        if n == 1:
            for part in (0, 1):
                near(s, part, 1)
                near(s, part, -1)
            for part in (0, 1):
                second(s, part, 0, 1)
                second(s, part, 0, -1)
        elif n == 2:
            for part in (0, 1):
                far(s, part)
            for part in (0, 1):
                for d in (1, -1):
                    second(s, part, d, 1)
                    second(s, part, d, -1)
            for part in (0, 1):
                last(s, part, 0)
        elif n == 3:
            for part in (0, 1):
                second(s, part, 2, 1)
                second(s, part, 2, -1)
            for part in (0, 1):
                last(s, part, 1)
                last(s, part, -1)
        else:
            for part in (0, 1):
                last(s, part, 2)

    half_copy(0).start()
    launch(0, 0)
    half_copy(1).start()

    cut = 112
    depth = samples_t.shape[0]
    low_f = pl.ds(pl.multiple_of(core * 256, 16), cut)
    high_f = pl.ds(pl.multiple_of(core * 256 + cut, 16), 256 - cut)
    sib_low = pl.ds(pl.multiple_of((1 - core) * 256, 16), cut)
    sib_high = pl.ds(pl.multiple_of((1 - core) * 256 + cut, 16), 256 - cut)
    x_samples = [
        remote(samples_t.at[low_f], peer_t.at[low_f], xs.at[2], xr.at[2], partner),
        remote(samples_t.at[high_f], peer_t.at[high_f], xs.at[3], xr.at[3], across),
    ]
    for cp in x_samples:
        cp.start()
    hand = [
        remote(peer_t.at[low_f], peer_t.at[low_f], hs.at[0], hr.at[0], sibling),
        remote(peer_t.at[high_f], peer_t.at[high_f], hs.at[1], hr.at[1], sibling),
    ]
    hand_in = [
        remote(peer_t.at[sib_low], peer_t.at[sib_low], hs.at[0], hr.at[0], sibling),
        remote(peer_t.at[sib_high], peer_t.at[sib_high], hs.at[1], hr.at[1], sibling),
    ]

    for i in (4, 5, 6):
        fetch[i].wait()
    xf = samples[...].astype(F32)
    sq = xf * xf
    sq_hi = sq.astype(BF16)
    sq_lo = (sq - sq_hi.astype(F32)).astype(BF16)
    ones = jnp.ones((16, depth), BF16)
    norm = (lax.dot_general(ones, sq_hi, NT, preferred_element_type=F32)
            + lax.dot_general(ones, sq_lo, NT, preferred_element_type=F32))
    w = weights[...]
    auxes[0] = jnp.where(iota((8, 1024), 0) == 0, w, -scale * norm[0:8])
    weighted[...] = (w * (targets[...] - preds[...])).astype(BF16)
    wt[:, 0:1024] = weighted[...]

    def weight_rows(half):
        v = auxes[half, 0:1]
        hi = v.astype(BF16).astype(F32)
        which = iota((16, 1024), 0)
        full = jnp.where(which == 0, hi, jnp.where(which == 1, v - hi, 0.0))
        wcat[:, half * 1024 : (half + 1) * 1024] = full.astype(BF16)

    weight_rows(0)
    x_rows = [
        remote(auxes.at[0], auxes.at[1], xs.at[4], xr.at[4], partner),
        remote(weighted, peer_wt, xs.at[5], xr.at[5], partner),
    ]
    for cp in x_rows:
        cp.start()

    half_copy(0).wait_recv()
    launch(0, 1)

    fetch[3].wait()
    parts = split3(coefs[...])
    for s in range(2):
        own_coef[s] = sum3(lax.dot_general(parts, select[s * 128 : (s + 1) * 128, :], NT,
                                           preferred_element_type=F32))
    x_coef = remote(own_coef, peer_coef, xs.at[6], xr.at[6], partner)
    x_coef.start()

    def l_copy(k):
        return remote(place, places.at[c], ls.at[k], lr.at[c], (r, lax.rem(c + k, 4)))

    def share_place(k, carry):
        l_copy(k).start()
        return carry

    lax.fori_loop(1, 4, share_place, 0)
    places[c] = place[...]

    def tiles(s, half, first, stop):
        src = samples_t if half == 0 else peer_t
        base = half * 1024

        def body(k, carry):
            g = lax.rem(z + k + k // 2 - 2 * (k // 3), 4)
            picked = cent[s, pl.ds(g * 4, 4)].reshape(384, 512)
            wide = picked.astype(F32)
            a = shift - scale * jnp.sum(wide * wide, axis=1, keepdims=True)
            for i in range(4):
                prod = jnp.dot(picked, src[:, i * 256 : (i + 1) * 256], preferred_element_type=F32)
                b = auxes[half, 1:2, i * 256 : (i + 1) * 256]
                val = jnp.exp2(prod * (2.0 * scale) + (a + b)).astype(BF16)
                lo = base + i * 256
                for q in range(4):
                    kt[s, g * 4 + q, 0:96, lo : lo + 256] = val[q * 96 : (q + 1) * 96]
            for q in (0, 2):
                k2 = kt[s, pl.ds(g * 4 + q, 2), :, base : base + 1024].reshape(256, 1024)
                part = lax.dot_general(wcat[:, base : base + 1024], k2 * k2, NT, preferred_element_type=F32)
                tot = jnp.broadcast_to(part[0:1] + part[1:2], (8, 256))
                for h in range(2):
                    now = tot[:, h * 128 : (h + 1) * 128]
                    if half == 0:
                        sqsend[s, g * 4 + q + h] = now
                    else:
                        sqsend[s, g * 4 + q + h] += now
            return carry

        lax.fori_loop(first, stop, body, 0)

    def s_copy(s, j):
        return remote(sqsend.at[s, j], sqrecv.at[s, me], ss.at[s, j], sr.at[s, me], plane_dev(j))

    def push_squares(s):
        def body(k, carry):
            s_copy(s, lax.rem(me + k, 16)).start()
            return carry

        lax.fori_loop(1, 16, body, 0)

    def g_copy(s, j):
        return remote(gsend.at[s, j], grecv.at[s, me], gs.at[s, j], gr.at[s, me], plane_dev(j))

    def gradient(s, lhs):
        def pair(j2):
            k = kt[s, pl.ds(j2 * 2, 2)].reshape(256, 2048)
            g = lax.dot_general(lhs, k, NT, preferred_element_type=F32).astype(BF16)
            gsend[s, j2 * 2] = g[:, 0:128]
            gsend[s, j2 * 2 + 1] = g[:, 128:256]

        def body(k, carry):
            j2 = lax.rem(me // 2 + k, 8)
            pair(j2)
            g_copy(s, j2 * 2).start()
            g_copy(s, j2 * 2 + 1).start()
            return carry

        lax.fori_loop(1, 8, body, 0)
        pair(me // 2)
        g_copy(s, me + 1 - 2 * lax.rem(me, 2)).start()

    def d_copy(s, j):
        return remote(dlow.at[s, me], dlow.at[s, me], ds_.at[s, j], dr.at[s, me], plane_dev(j))

    def f_copy(s, k):
        return remote(dall.at[s, e], dall.at[s, e], fs.at[s, k], fr.at[s, e], ring_dev(k))

    def make_delta(s):
        def square(k, total):
            j = lax.rem(me + k, 16)
            remote(sqsend.at[s, j], sqrecv.at[s, j], ss.at[s, j], sr.at[s, j], plane_dev(j)).wait_recv()
            return total + sqrecv[s, j]

        lane = iota((16, 128), 1)
        coef = jnp.where(lane < 48, own_coef[s], peer_coef[s])
        col_square = lax.fori_loop(1, 16, square, sqsend[s, me])
        inverse = 1.0 / (col_square[0:1] + RIDGE)

        def body(k, total):
            j = lax.rem(me + k, 16)
            remote(gsend.at[s, j], grecv.at[s, j], gs.at[s, j], gr.at[s, j], plane_dev(j)).wait_recv()
            return total + grecv[s, j].astype(F32)

        total = lax.fori_loop(1, 16, body, gsend[s, me].astype(F32) - RIDGE * coef)
        delta = total * inverse
        dlow[s, me] = delta.astype(BF16)
        dall[s, e] = delta

        def push(k, carry):
            d_copy(s, lax.rem(me + k, 16)).start()
            return carry

        lax.fori_loop(1, 16, push, 0)

    def push_delta(s):
        def push_ring(k, carry):
            f_copy(s, lax.rem(e + k, 8)).start()
            return carry

        lax.fori_loop(1, 8, push_ring, 0)

    def wait_delta(s):
        def body(k, carry):
            j = lax.rem(me + k, 16)
            remote(dlow.at[s, j], dlow.at[s, j], ds_.at[s, j], dr.at[s, j], plane_dev(j)).wait_recv()
            return carry

        lax.fori_loop(1, 16, body, 0)
        return jnp.concatenate([dlow[s, j] for j in range(16)], axis=1)

    def p_copy(to):
        return remote(psend.at[to], precv.at[e], ps.at[to], pr.at[e], ring_dev(to))

    def change(d):
        def chunk(to):
            rel = lax.rem(to // 4 + xl, 2) * 4 + lax.rem(to, 4)
            k = kt[0, :, :, pl.ds(pl.multiple_of(rel * 256, 256), 256)].reshape(2048, 256)
            psend[to] = jnp.dot(d, k, preferred_element_type=F32).astype(BF16)

        def body(k, carry):
            to = lax.rem(e + k, 8)
            chunk(to)
            p_copy(to).start()
            return carry

        lax.fori_loop(1, 8, body, 0)
        chunk(e)

    def sum_change():
        def body(k, total):
            j = lax.rem(e + k, 8)
            remote(psend.at[j], precv.at[j], ps.at[j], pr.at[j], ring_dev(j)).wait_recv()
            return total + precv[j].astype(F32)

        return lax.fori_loop(1, 8, body, psend[e].astype(F32))

    def update_coefs(s, base):
        def body(k, carry):
            j = lax.rem(e + k, 8)
            remote(dall.at[s, j], dall.at[s, j], fs.at[s, j], fr.at[s, j], ring_dev(j)).wait_recv()
            return carry

        lax.fori_loop(1, 8, body, 0)
        lane = iota((16, 128), 1)
        pieces, cols = [], []
        for k in range(4):
            own = dall[s, xl * 4 + k]
            other = dall[s, (1 - xl) * 4 + k]
            pieces.append(jnp.where(lane < 48, own, other))
            cols.append(jnp.broadcast_to(places[k, s, 0:1], (128, 128)).T)
        lhs = split3(jnp.concatenate(pieces, axis=1))
        col = jnp.concatenate(cols, axis=0)

        def step(k, carry):
            at = pl.ds(pl.multiple_of(k * 512, 512), 512)
            base_lane = (k * 512).astype(F32)
            hot = []
            for i in range(4):
                lanes = iota((512, 128), 1).astype(F32) + (base_lane + i * 128.0)
                hot.append((col == lanes).astype(F32).astype(BF16))
            three = jnp.dot(lhs, jnp.concatenate(hot, axis=1), preferred_element_type=F32)
            coef_out[:, at] = base[:, at] + sum3(three)
            return carry

        lax.fori_loop(0, 8, step, 0)

    for s in range(2):
        for j in range(16):
            kt[s, j, 96:128, :] = jnp.zeros((32, 2048), BF16)
    level(0, 1)
    level(0, 2)
    launch(1, 0)
    half_copy(1).wait_recv()
    launch(1, 1)
    tiles(0, 0, 0, 1)
    level(0, 3)
    for i in range(2):
        x_samples[i].wait_recv()
        hand[i].start()
    tiles(0, 0, 1, 3)
    level(0, 4)
    level(1, 1)
    tiles(0, 0, 3, 4)
    x_rows[0].wait_recv()
    x_rows[1].wait_recv()
    weight_rows(1)
    wt[:, 1024:2048] = peer_wt[...]
    for i in range(2):
        hand_in[i].wait_recv()
    tiles(0, 1, 0, 4)
    push_squares(0)
    level(1, 2)
    gradient(0, wt[...])
    tiles(1, 0, 0, 1)
    level(1, 3)
    tiles(1, 0, 1, 3)
    x_coef.wait_recv()
    make_delta(0)
    push_delta(0)
    level(1, 4)
    tiles(1, 0, 3, 4)
    tiles(1, 1, 0, 2)
    change(wait_delta(0))
    tiles(1, 1, 2, 3)
    chunk_at = pl.ds(pl.multiple_of(c * 256, 256), 256)
    pred = preds[:, chunk_at] + sum_change()

    def rel_to(to):
        return lax.rem(to // 4 + xl, 2) * 4 + c

    def w_copy(to):
        return remote(wt2.at[c], wt2.at[rel_to(to)], ws.at[to], wr.at[rel_to(to)], ring_dev(to))

    wt2[c] = (weights[:, chunk_at] * (targets[:, chunk_at] - pred)).astype(BF16)

    def push_w(k, carry):
        w_copy(lax.rem(e + k, 8)).start()
        return carry

    lax.fori_loop(1, 8, push_w, 0)
    pmid[c] = pred

    def q_copy(k):
        to = lax.rem(c + k, 4)
        return remote(pmid.at[c], pmid.at[c], qs.at[to], qr.at[c], (r, to))

    def push_q(k, carry):
        q_copy(k).start()
        return carry

    tiles(1, 1, 3, 4)
    push_squares(1)

    def wait_w(k, carry):
        j = lax.rem(c + k, 8)
        remote(wt2.at[j], wt2.at[j], ws.at[j], wr.at[j], ring_dev(j)).wait_recv()
        return carry

    lax.fori_loop(1, 8, wait_w, 0)
    gradient(1, jnp.concatenate([wt2[j] for j in range(8)], axis=1))
    lax.fori_loop(1, 4, push_q, 0)

    def wait_place(k, carry):
        j = lax.rem(c + k, 4)
        remote(place, places.at[j], ls.at[k], lr.at[j], (r, j)).wait_recv()
        return carry

    lax.fori_loop(1, 4, wait_place, 0)
    update_coefs(0, coefs)
    make_delta(1)
    push_delta(1)
    d = wait_delta(1)

    def e_copy(rel, half, across_x):
        to_xl = xl if rel == 0 else 1 - xl
        to_hi = c // 2 if across_x == 0 else 1 - c // 2
        n = (rel * 2 + half) * 2 + across_x
        dev = (to_xl * 16 + me, to_hi * 2 + half)
        return remote(lsend.at[rel * 2 + half], lrecv.at[e], es.at[n], er.at[e], dev)

    for rel in (1, 0):
        for half in range(2):
            k = kt[1, :, :, rel * 1024 + half * 512 : rel * 1024 + half * 512 + 512].reshape(2048, 512)
            lsend[rel * 2 + half] = jnp.dot(d, k, preferred_element_type=F32).astype(BF16)
            e_copy(rel, half, 1).start()
            if rel == 1:
                e_copy(rel, half, 0).start()
            else:
                pl.when(core != half)(lambda half=half: e_copy(0, half, 0).start())
    lrecv[e] = lsend[core]
    update_coefs(1, coef_out)

    def wait_q(k, carry):
        j = lax.rem(c + k, 4)
        remote(pmid.at[j], pmid.at[j], qs.at[j], qr.at[j], (r, j)).wait_recv()
        return carry

    lax.fori_loop(1, 4, wait_q, 0)

    def wait_e(k, carry):
        j = lax.rem(e + k, 8)
        remote(lrecv.at[j], lrecv.at[j], es.at[0], er.at[j], ring_dev(j)).wait_recv()
        return carry

    lax.fori_loop(1, 8, wait_e, 0)
    total = lrecv[0].astype(F32)
    for j in range(1, 8):
        total = total + lrecv[j].astype(F32)
    pend[core] = jnp.concatenate([pmid[core * 2], pmid[core * 2 + 1]], axis=1) + total
    final = remote(pend.at[core], pend.at[core], hs.at[2], hr.at[2], sibling)
    final.start()
    remote(pend.at[1 - core], pend.at[1 - core], hs.at[2], hr.at[2], sibling).wait_recv()
    pred_out[:, 0:512] = pend[0]
    pred_out[:, 512:1024] = pend[1]

    for s in range(2):
        half_copy(s).wait_send()
        for cp in started[s]:
            cp.wait_send()
    for cp in (*x_samples, *x_rows, x_coef, *hand, final):
        cp.wait_send()

    def drain_plane(k, carry):
        j = lax.rem(me + k, 16)
        for s in range(2):
            g_copy(s, j).wait_send()
            s_copy(s, j).wait_send()
            d_copy(s, j).wait_send()
        return carry

    def drain_ring(k, carry):
        j = lax.rem(e + k, 8)
        for s in range(2):
            f_copy(s, j).wait_send()
        p_copy(j).wait_send()
        w_copy(j).wait_send()
        return carry

    def drain_cent(k, carry):
        q_copy(k).wait_send()
        l_copy(k).wait_send()
        return carry

    lax.fori_loop(1, 16, drain_plane, 0)
    lax.fori_loop(1, 8, drain_ring, 0)
    lax.fori_loop(1, 4, drain_cent, 0)
    for rel in range(2):
        for half in range(2):
            e_copy(rel, half, 1).wait_send()
            if rel == 1:
                e_copy(rel, half, 0).wait_send()
            else:
                pl.when(core != half)(lambda half=half: e_copy(0, half, 0).wait_send())


def local(samples, weights, targets, predictions, centres, coefs, block_index):
    rows, depth = samples.shape
    pool = centres.shape[0]
    t = targets.shape[0]
    sharpness = 1.3 / math.sqrt(8.0 * depth)
    offset = 2.0 * depth * sharpness - 1.5 - 0.5 * math.log(rows * lax.axis_size("rows"))
    scale = sharpness * LOG2E
    shift = offset * LOG2E
    vmem = pl.BlockSpec(memory_space=pltpu.VMEM)
    hbm = pl.BlockSpec(memory_space=pl.ANY)
    sds = jax.ShapeDtypeStruct
    dma = pltpu.SemaphoreType.DMA
    pred, coef = pl.pallas_call(
        functools.partial(main_kernel, scale, shift),
        out_shape=(sds((t, rows), F32), sds((t, pool), F32)),
        in_specs=[hbm] * 7,
        out_specs=(vmem,) * 2,
        scratch_shapes=[
            pltpu.VMEM(block_index.shape, jnp.int32),
            pltpu.VMEM(centres.shape, BF16),
            pltpu.VMEM(coefs.shape, F32),
            pltpu.VMEM(samples.shape, BF16),
            pltpu.VMEM((1, rows), F32),
            pltpu.VMEM((t, rows), F32),
            pltpu.VMEM((t, rows), F32),
            pltpu.VMEM((256, pool), BF16),
            pltpu.VMEM((2, 48, depth), BF16),
            pltpu.VMEM((2, t, 128), F32),
            pltpu.VMEM((2, 8, 128), F32),
            pltpu.VMEM((t, rows), BF16),
            pltpu.VMEM((depth, rows), BF16),
            pltpu.VMEM((2, 16, 96, depth), BF16),
            pltpu.VMEM((depth, rows), BF16),
            pltpu.VMEM((2, t, 128), F32),
            pltpu.VMEM((4, 2, 8, 128), F32),
            pltpu.VMEM((t, 2 * rows), BF16),
            pltpu.VMEM((t, rows), BF16),
            pltpu.VMEM((2, 8, rows), F32),
            pltpu.VMEM((16, 2 * rows), BF16),
            pltpu.VMEM((2, 16, 128, 2 * rows), BF16),
            pltpu.VMEM((2, 16, t, 128), BF16),
            pltpu.VMEM((2, 16, t, 128), BF16),
            pltpu.VMEM((2, 16, 8, 128), F32),
            pltpu.VMEM((2, 16, 8, 128), F32),
            pltpu.VMEM((2, 16, t, 128), BF16),
            pltpu.VMEM((2, 8, t, 128), F32),
            pltpu.VMEM((8, t, 256), BF16),
            pltpu.VMEM((8, t, 256), BF16),
            pltpu.VMEM((4, t, 512), BF16),
            pltpu.VMEM((8, t, 512), BF16),
            pltpu.VMEM((8, t, 256), BF16),
            pltpu.VMEM((4, t, 256), F32),
            pltpu.VMEM((2, t, 512), F32),
            dma((7,)),
            dma((7,)), dma((7,)),
            dma((2, 30)), dma((2, 2, 16)),
            dma((2, 16)), dma((2, 16)),
            dma((2, 16)), dma((2, 16)),
            dma((2, 16)), dma((2, 16)),
            dma((2, 8)), dma((2, 8)),
            dma((8,)), dma((8,)),
            dma((8,)), dma((8,)),
            dma((8,)), dma((8,)),
            dma((4,)), dma((4,)),
            dma((4,)), dma((4,)),
            dma((3,)), dma((3,)),
        ],
        compiler_params=pltpu.CompilerParams(
            collective_id=0, has_side_effects=True, vmem_limit_bytes=60 * 2**20
        ),
    )(block_index, centres, coefs, samples, weights[None, :], targets, predictions)
    return coef, pred


def solution(mesh):
    in_specs = (
        P("rows", None),
        P("rows"),
        P(None, "rows"),
        P(None, "rows"),
        P("rows", None),
        P(None, "rows"),
        P(None, "cent"),
    )
    out_specs = (P(None, "rows"), P(None, "rows"))
    return jax.shard_map(local, mesh=mesh, in_specs=in_specs, out_specs=out_specs, check_vma=False)
```

time: 106 us -> 82.7 us (0.78)
  Pallas kernels: 96.3 us -> 78.7 us
  local copies, waits for them, and re-layouts: 8.81 us -> 3.14 us
    pallas_call x1, Pallas kernels: 93.5 us -> 78.7 us  [local(): pl.pallas_call(functools.partial(main_kernel, scale, shift), out_shape=(s...]
    unnamed x21 -> x2, local copies, waits for them, and re-layouts: 8.81 us -> 3.14 us
    pallas_call x1 -> x0, Pallas kernels: 2.85 us -> none  [local(): pl.pallas_call(functools.partial(extract, scale), out_shape=(sds((2, 96,...]
where the time goes in v2:
time: 82.7 us; the launch traced here: 82.5 us
  Pallas kernels  78.7 us (95%)
  local copies, waits for them, and re-layouts  3.14 us (4%)
    pallas_call x1, Pallas kernels, local(): pl.pallas_call(functools.partial(main_kernel, scale, shift), out_shape=(s...  78.7 us
    unnamed x2, local copies, waits for them, and re-layouts  3.14 us

profile of v2, /device:TPU:1, one launch (start us, length us, event | category | flops | bytes accessed | tf_op | source)
XLA Modules:
  0.0 82.5 jit_solution(16555256624748367182)
XLA Ops:
  0.6 78.7 %shard_map.86 = (f32[16,1024]{1,0:T(8,128)}, f32[16,4096]{1,0:T(8,128)}) custom-call(s32[2,3072]{1,0:T(2,128)} %blk_in.1, bf16[4096,512]{1,0:T(8,128)(2,1)} %centres_in.1, f32[16,4096]{1,0:T(8,128)} %coefs_in.1, bf16[1024,512]{1,0:T(8,128)(2,1)} %samples_in.1, f32[1,1024]{1,0:T(1,128)} %bitcast.1, f32[16,1024]{1,0:T(8,128)} %targets_in.1, f32[16,1024]{1,0:T(8,128)} %preds_in.1), custom_call_target="tpu_custom_call" | custom-call | tf_op jit(solution)/shard_map/pallas_call | solution.py:621
  79.3 1.7 %copy.11 = f32[16,4096]{1,0:T(8,128)} copy(f32[16,4096]{1,0:T(8,128)} %get-tuple-element.8) | data formatting | bytes 524288
  81.0 1.5 %copy.12 = f32[16,1024]{1,0:T(8,128)} copy(f32[16,1024]{1,0:T(8,128)} %get-tuple-element.9) | data formatting | bytes 131072

commit v3 on v2

--- a/solution.py
+++ b/solution.py
@@ -32,7 +32,7 @@
 
 
 def main_kernel(scale, shift, blk_in, centres_in, coefs_in, samples_in, weights_in, targets_in, preds_in,
-                pred_out, coef_out,
+                pred_hbm, coef_hbm, pred_out, coef_out,
                 blk, centres, coefs, samples, weights, targets, preds, select,
                 outgoing, own_coef, place, weighted, samples_t,
                 cent, peer_t, peer_coef, places, wt, peer_wt, auxes, wcat, kt, gsend, grecv, sqsend, sqrecv,
@@ -51,6 +51,17 @@
     def wrap(v):
         return lax.rem(v + 8, 4)
 
+    def offset_of(i):
+        return 2 - i + 3 * (i // 2) - 2 * (i // 3)
+
+    def peer_of(k):
+        return wrap(z + offset_of(k // 4)) * 4 + wrap(y + offset_of(lax.rem(k, 4)))
+
+    def ring_of(k):
+        m = k + 2 - 7 * (k // 6) - 2 * (k // 7)
+        hi = lax.rem(c // 2 + m // 2, 2)
+        return lax.rem(xl + m // 4, 2) * 4 + hi * 2 + lax.rem(c + m, 2)
+
     def plane_dev(j):
         return (xl * 16 + j, c)
 
@@ -65,16 +76,17 @@
 
     barrier = pltpu.get_barrier_semaphore()
 
-    def greet_plane(k, carry):
-        pl.semaphore_signal(barrier, inc=1, device_id=plane_dev(lax.rem(me + k, 16)), device_id_type=MESH)
-        return carry
-
-    def greet_ring(k, carry):
-        pl.semaphore_signal(barrier, inc=1, device_id=ring_dev(lax.rem(e + k, 8)), device_id_type=MESH)
-        return carry
-
-    lax.fori_loop(1, 16, greet_plane, 0)
-    lax.fori_loop(1, 8, greet_ring, 0)
+    neighbours = (
+        plane_dev(z * 4 + wrap(y + 1)),
+        plane_dev(z * 4 + wrap(y - 1)),
+        plane_dev(wrap(z + 1) * 4 + y),
+        plane_dev(wrap(z - 1) * 4 + y),
+        ((1 - xl) * 16 + me, c),
+        ((1 - xl) * 16 + me, lax.rem(c + 2, 4)),
+        (r, c + 1 - 2 * core),
+    )
+    for dev in neighbours:
+        pl.semaphore_signal(barrier, inc=1, device_id=dev, device_id_type=MESH)
 
     pool = centres.shape[0]
     q_rows = blk.shape[1] // 128
@@ -108,7 +120,7 @@
     fetch[2].wait()
     samples_t[...] = samples[...].T
 
-    pl.semaphore_wait(barrier, 22)
+    pl.semaphore_wait(barrier, len(neighbours))
 
     def remote(src, dst, ssem, rsem, dev):
         return pltpu.make_async_remote_copy(src_ref=src, dst_ref=dst, send_sem=ssem, recv_sem=rsem,
@@ -168,33 +180,25 @@
     def last(s, part, d):
         got(s, part, slot(part, d, 2))
 
-    def level(s, n):
+    def level(s, part, n):
         if n == 1:
-            for part in (0, 1):
-                near(s, part, 1)
-                near(s, part, -1)
-            for part in (0, 1):
-                second(s, part, 0, 1)
-                second(s, part, 0, -1)
+            near(s, part, 1)
+            near(s, part, -1)
+            second(s, part, 0, 1)
+            second(s, part, 0, -1)
         elif n == 2:
-            for part in (0, 1):
-                far(s, part)
-            for part in (0, 1):
-                for d in (1, -1):
-                    second(s, part, d, 1)
-                    second(s, part, d, -1)
-            for part in (0, 1):
-                last(s, part, 0)
+            far(s, part)
+            for d in (1, -1):
+                second(s, part, d, 1)
+                second(s, part, d, -1)
+            last(s, part, 0)
         elif n == 3:
-            for part in (0, 1):
-                second(s, part, 2, 1)
-                second(s, part, 2, -1)
-            for part in (0, 1):
-                last(s, part, 1)
-                last(s, part, -1)
+            second(s, part, 2, 1)
+            second(s, part, 2, -1)
+            last(s, part, 1)
+            last(s, part, -1)
         else:
-            for part in (0, 1):
-                last(s, part, 2)
+            last(s, part, 2)
 
     half_copy(0).start()
     launch(0, 0)
@@ -268,7 +272,6 @@
         l_copy(k).start()
         return carry
 
-    lax.fori_loop(1, 4, share_place, 0)
     places[c] = place[...]
 
     def tiles(s, half, first, stop):
@@ -322,13 +325,13 @@
             gsend[s, j2 * 2 + 1] = g[:, 128:256]
 
         def body(k, carry):
-            j2 = lax.rem(me // 2 + k, 8)
+            j2 = wrap(z + offset_of(k // 2)) * 2 + lax.rem(y // 2 + 1 + k, 2)
             pair(j2)
             g_copy(s, j2 * 2).start()
             g_copy(s, j2 * 2 + 1).start()
             return carry
 
-        lax.fori_loop(1, 8, body, 0)
+        lax.fori_loop(0, 7, body, 0)
         pair(me // 2)
         g_copy(s, me + 1 - 2 * lax.rem(me, 2)).start()
 
@@ -360,10 +363,10 @@
         dall[s, e] = delta
 
         def push(k, carry):
-            d_copy(s, lax.rem(me + k, 16)).start()
-            return carry
-
-        lax.fori_loop(1, 16, push, 0)
+            d_copy(s, peer_of(k)).start()
+            return carry
+
+        lax.fori_loop(0, 15, push, 0)
 
     def push_delta(s):
         def push_ring(k, carry):
@@ -391,12 +394,12 @@
             psend[to] = jnp.dot(d, k, preferred_element_type=F32).astype(BF16)
 
         def body(k, carry):
-            to = lax.rem(e + k, 8)
+            to = ring_of(k)
             chunk(to)
             p_copy(to).start()
             return carry
 
-        lax.fori_loop(1, 8, body, 0)
+        lax.fori_loop(0, 7, body, 0)
         chunk(e)
 
     def sum_change():
@@ -437,44 +440,55 @@
 
         lax.fori_loop(0, 8, step, 0)
 
+    level(0, 0, 1)
     for s in range(2):
         for j in range(16):
             kt[s, j, 96:128, :] = jnp.zeros((32, 2048), BF16)
-    level(0, 1)
-    level(0, 2)
+    level(0, 0, 2)
+    level(0, 1, 1)
+    level(0, 0, 3)
+    level(0, 1, 2)
+    tiles(0, 0, 0, 1)
     launch(1, 0)
     half_copy(1).wait_recv()
     launch(1, 1)
-    tiles(0, 0, 0, 1)
-    level(0, 3)
+    level(0, 0, 4)
+    level(0, 1, 3)
     for i in range(2):
         x_samples[i].wait_recv()
         hand[i].start()
     tiles(0, 0, 1, 3)
-    level(0, 4)
-    level(1, 1)
-    tiles(0, 0, 3, 4)
+    level(1, 0, 1)
+    level(1, 1, 1)
     x_rows[0].wait_recv()
     x_rows[1].wait_recv()
     weight_rows(1)
     wt[:, 1024:2048] = peer_wt[...]
     for i in range(2):
         hand_in[i].wait_recv()
-    tiles(0, 1, 0, 4)
+    lax.fori_loop(1, 4, share_place, 0)
+    tiles(0, 1, 0, 3)
+    level(0, 1, 4)
+    tiles(0, 0, 3, 4)
+    tiles(0, 1, 3, 4)
     push_squares(0)
-    level(1, 2)
     gradient(0, wt[...])
+    level(1, 0, 2)
+    level(1, 1, 2)
     tiles(1, 0, 0, 1)
-    level(1, 3)
-    tiles(1, 0, 1, 3)
+    tiles(1, 1, 0, 1)
     x_coef.wait_recv()
     make_delta(0)
+    level(1, 0, 3)
+    level(1, 1, 3)
     push_delta(0)
-    level(1, 4)
+    tiles(1, 0, 1, 3)
+    tiles(1, 1, 1, 2)
+    change(wait_delta(0))
+    level(1, 0, 4)
+    level(1, 1, 4)
+    tiles(1, 1, 2, 3)
     tiles(1, 0, 3, 4)
-    tiles(1, 1, 0, 2)
-    change(wait_delta(0))
-    tiles(1, 1, 2, 3)
     chunk_at = pl.ds(pl.multiple_of(c * 256, 256), 256)
     pred = preds[:, chunk_at] + sum_change()
 
@@ -487,10 +501,10 @@
     wt2[c] = (weights[:, chunk_at] * (targets[:, chunk_at] - pred)).astype(BF16)
 
     def push_w(k, carry):
-        w_copy(lax.rem(e + k, 8)).start()
-        return carry
-
-    lax.fori_loop(1, 8, push_w, 0)
+        w_copy(ring_of(k)).start()
+        return carry
+
+    lax.fori_loop(0, 7, push_w, 0)
     pmid[c] = pred
 
     def q_copy(k):
@@ -531,7 +545,7 @@
         dev = (to_xl * 16 + me, to_hi * 2 + half)
         return remote(lsend.at[rel * 2 + half], lrecv.at[e], es.at[n], er.at[e], dev)
 
-    for rel in (1, 0):
+    for rel in range(2):
         for half in range(2):
             k = kt[1, :, :, rel * 1024 + half * 512 : rel * 1024 + half * 512 + 512].reshape(2048, 512)
             lsend[rel * 2 + half] = jnp.dot(d, k, preferred_element_type=F32).astype(BF16)
@@ -542,6 +556,8 @@
                 pl.when(core != half)(lambda half=half: e_copy(0, half, 0).start())
     lrecv[e] = lsend[core]
     update_coefs(1, coef_out)
+    store_coef = pltpu.make_async_copy(coef_out, coef_hbm, loads.at[7])
+    store_coef.start()
 
     def wait_q(k, carry):
         j = lax.rem(c + k, 4)
@@ -566,6 +582,8 @@
     pred_out[:, 0:512] = pend[0]
     pred_out[:, 512:1024] = pend[1]
 
+    store_pred = pltpu.make_async_copy(pred_out, pred_hbm, loads.at[8])
+    store_pred.start()
     for s in range(2):
         half_copy(s).wait_send()
         for cp in started[s]:
@@ -594,6 +612,7 @@
         l_copy(k).wait_send()
         return carry
 
+    store_coef.wait()
     lax.fori_loop(1, 16, drain_plane, 0)
     lax.fori_loop(1, 8, drain_ring, 0)
     lax.fori_loop(1, 4, drain_cent, 0)
@@ -604,6 +623,7 @@
                 e_copy(rel, half, 0).wait_send()
             else:
                 pl.when(core != half)(lambda half=half: e_copy(0, half, 0).wait_send())
+    store_pred.wait()
 
 
 def local(samples, weights, targets, predictions, centres, coefs, block_index):
@@ -622,8 +642,10 @@
         functools.partial(main_kernel, scale, shift),
         out_shape=(sds((t, rows), F32), sds((t, pool), F32)),
         in_specs=[hbm] * 7,
-        out_specs=(vmem,) * 2,
+        out_specs=(hbm,) * 2,
         scratch_shapes=[
+            pltpu.VMEM((t, rows), F32),
+            pltpu.VMEM((t, pool), F32),
             pltpu.VMEM(block_index.shape, jnp.int32),
             pltpu.VMEM(centres.shape, BF16),
             pltpu.VMEM(coefs.shape, F32),
@@ -659,7 +681,7 @@
             pltpu.VMEM((8, t, 256), BF16),
             pltpu.VMEM((4, t, 256), F32),
             pltpu.VMEM((2, t, 512), F32),
-            dma((7,)),
+            dma((9,)),
             dma((7,)), dma((7,)),
             dma((2, 30)), dma((2, 2, 16)),
             dma((2, 16)), dma((2, 16)),

time: 82.7 us -> 80.5 us (0.973)
  Pallas kernels: 78.7 us -> 76.6 us
    pallas_call x1, Pallas kernels: 78.7 us -> 76.6 us  [local(): pl.pallas_call(functools.partial(main_kernel, scale, shift), out_shape=(s...]
where the time goes in v3:
time: 80.5 us; the launch traced here: 80.4 us
  Pallas kernels  76.6 us (95%)
  local copies, waits for them, and re-layouts  3.14 us (4%)
    pallas_call x1, Pallas kernels, local(): pl.pallas_call(functools.partial(main_kernel, scale, shift), out_shape=(s...  76.6 us
    unnamed x2, local copies, waits for them, and re-layouts  3.14 us

profile of v3, /device:TPU:1, one launch (start us, length us, event | category | flops | bytes accessed | tf_op | source)
XLA Modules:
  0.0 80.4 jit_solution(4382419790441749943)
XLA Ops:
  0.6 76.6 %shard_map.86 = (f32[16,1024]{1,0:T(8,128)}, f32[16,4096]{1,0:T(8,128)}) custom-call(s32[2,3072]{1,0:T(2,128)} %blk_in.1, bf16[4096,512]{1,0:T(8,128)(2,1)} %centres_in.1, f32[16,4096]{1,0:T(8,128)} %coefs_in.1, bf16[1024,512]{1,0:T(8,128)(2,1)} %samples_in.1, f32[1,1024]{1,0:T(1,128)} %bitcast.1, f32[16,1024]{1,0:T(8,128)} %targets_in.1, f32[16,1024]{1,0:T(8,128)} %preds_in.1), custom_call_target="tpu_custom_call" | custom-call | tf_op jit(solution)/shard_map/pallas_call | solution.py:641
  77.2 1.7 %copy.11 = f32[16,4096]{1,0:T(8,128)} copy(f32[16,4096]{1,0:T(8,128)} %get-tuple-element.8) | data formatting | bytes 524288
  78.9 1.5 %copy.12 = f32[16,1024]{1,0:T(8,128)} copy(f32[16,1024]{1,0:T(8,128)} %get-tuple-element.9) | data formatting | bytes 131072

commit v4 on v3

--- a/solution.py
+++ b/solution.py
@@ -9,6 +9,7 @@
 from jax.sharding import PartitionSpec as P
 
 RIDGE = 1.0
+KEEP = 64
 MESH = pl.DeviceIdType.MESH
 F32, BF16 = jnp.float32, jnp.bfloat16
 LOG2E = 1.4426950408889634
@@ -115,8 +116,8 @@
     fetch[1].wait()
     rows = jnp.dot(select[...], centres[...], preferred_element_type=F32).astype(BF16)
     for s in range(2):
-        cent[s, me, 0:48] = rows[s * 128 : s * 128 + 48]
-        outgoing[s] = rows[s * 128 + 48 : s * 128 + 96]
+        cent[s, me, 0:KEEP] = rows[s * 128 : s * 128 + KEEP]
+        outgoing[s] = rows[s * 128 + KEEP : s * 128 + 96]
     fetch[2].wait()
     samples_t[...] = samples[...].T
 
@@ -131,7 +132,7 @@
     sibling = (r, c + 1 - 2 * core)
 
     def half_copy(s):
-        return remote(outgoing.at[s], cent.at[s, me, pl.ds(48, 48)], xs.at[s], xr.at[s], partner)
+        return remote(outgoing.at[s], cent.at[s, me, pl.ds(KEEP, 96 - KEEP)], xs.at[s], xr.at[s], partner)
 
     counters = [0, 0]
     started = [[], []]
@@ -144,13 +145,13 @@
     def send(s, part, j, a, b):
         n = counters[s]
         counters[s] += 1
-        ref = cent.at[s, j, pl.ds(48 * part, 48)]
+        ref = cent.at[s, j, pl.ds(KEEP * part, 96 - KEEP if part else KEEP)]
         cp = remote(ref, ref, cs.at[s, n], cr.at[s, part, j], plane_dev(slot(part, a, b)))
         cp.start()
         started[s].append(cp)
 
     def got(s, part, j):
-        ref = cent.at[s, j, pl.ds(48 * part, 48)]
+        ref = cent.at[s, j, pl.ds(KEEP * part, 96 - KEEP if part else KEEP)]
         remote(ref, ref, cs.at[s, 0], cr.at[s, part, j], plane_dev(slot(part, 1, 0))).wait_recv()
 
     def launch(s, part):
@@ -348,7 +349,7 @@
             return total + sqrecv[s, j]
 
         lane = iota((16, 128), 1)
-        coef = jnp.where(lane < 48, own_coef[s], peer_coef[s])
+        coef = jnp.where(lane < KEEP, own_coef[s], peer_coef[s])
         col_square = lax.fori_loop(1, 16, square, sqsend[s, me])
         inverse = 1.0 / (col_square[0:1] + RIDGE)
 
@@ -422,7 +423,7 @@
         for k in range(4):
             own = dall[s, xl * 4 + k]
             other = dall[s, (1 - xl) * 4 + k]
-            pieces.append(jnp.where(lane < 48, own, other))
+            pieces.append(jnp.where(lane < KEEP, own, other))
             cols.append(jnp.broadcast_to(places[k, s, 0:1], (128, 128)).T)
         lhs = split3(jnp.concatenate(pieces, axis=1))
         col = jnp.concatenate(cols, axis=0)
@@ -453,10 +454,10 @@
     half_copy(1).wait_recv()
     launch(1, 1)
     level(0, 0, 4)
-    level(0, 1, 3)
     for i in range(2):
         x_samples[i].wait_recv()
         hand[i].start()
+    level(0, 1, 3)
     tiles(0, 0, 1, 3)
     level(1, 0, 1)
     level(1, 1, 1)
@@ -534,6 +535,37 @@
 
     lax.fori_loop(1, 4, wait_place, 0)
     update_coefs(0, coefs)
+    for s in range(2):
+        half_copy(s).wait_send()
+        for cp in started[s]:
+            cp.wait_send()
+    for cp in (*x_samples, *x_rows, x_coef, *hand):
+        cp.wait_send()
+
+    def drain_plane(s):
+        def body(k, carry):
+            j = lax.rem(me + k, 16)
+            g_copy(s, j).wait_send()
+            s_copy(s, j).wait_send()
+            d_copy(s, j).wait_send()
+            return carry
+
+        lax.fori_loop(1, 16, body, 0)
+
+    def drain_ring(k, carry):
+        j = lax.rem(e + k, 8)
+        f_copy(0, j).wait_send()
+        p_copy(j).wait_send()
+        w_copy(j).wait_send()
+        return carry
+
+    def drain_cent(k, carry):
+        l_copy(k).wait_send()
+        return carry
+
+    drain_plane(0)
+    lax.fori_loop(1, 8, drain_ring, 0)
+    lax.fori_loop(1, 4, drain_cent, 0)
     make_delta(1)
     push_delta(1)
     d = wait_delta(1)
@@ -558,6 +590,17 @@
     update_coefs(1, coef_out)
     store_coef = pltpu.make_async_copy(coef_out, coef_hbm, loads.at[7])
     store_coef.start()
+    def drain_last(k, carry):
+        f_copy(1, lax.rem(e + k, 8)).wait_send()
+        return carry
+
+    def drain_mid(k, carry):
+        q_copy(k).wait_send()
+        return carry
+
+    drain_plane(1)
+    lax.fori_loop(1, 8, drain_last, 0)
+    lax.fori_loop(1, 4, drain_mid, 0)
 
     def wait_q(k, carry):
         j = lax.rem(c + k, 4)
@@ -584,38 +627,6 @@
 
     store_pred = pltpu.make_async_copy(pred_out, pred_hbm, loads.at[8])
     store_pred.start()
-    for s in range(2):
-        half_copy(s).wait_send()
-        for cp in started[s]:
-            cp.wait_send()
-    for cp in (*x_samples, *x_rows, x_coef, *hand, final):
-        cp.wait_send()
-
-    def drain_plane(k, carry):
-        j = lax.rem(me + k, 16)
-        for s in range(2):
-            g_copy(s, j).wait_send()
-            s_copy(s, j).wait_send()
-            d_copy(s, j).wait_send()
-        return carry
-
-    def drain_ring(k, carry):
-        j = lax.rem(e + k, 8)
-        for s in range(2):
-            f_copy(s, j).wait_send()
-        p_copy(j).wait_send()
-        w_copy(j).wait_send()
-        return carry
-
-    def drain_cent(k, carry):
-        q_copy(k).wait_send()
-        l_copy(k).wait_send()
-        return carry
-
-    store_coef.wait()
-    lax.fori_loop(1, 16, drain_plane, 0)
-    lax.fori_loop(1, 8, drain_ring, 0)
-    lax.fori_loop(1, 4, drain_cent, 0)
     for rel in range(2):
         for half in range(2):
             e_copy(rel, half, 1).wait_send()
@@ -623,6 +634,8 @@
                 e_copy(rel, half, 0).wait_send()
             else:
                 pl.when(core != half)(lambda half=half: e_copy(0, half, 0).wait_send())
+    final.wait_send()
+    store_coef.wait()
     store_pred.wait()
 
 
@@ -654,7 +667,7 @@
             pltpu.VMEM((t, rows), F32),
             pltpu.VMEM((t, rows), F32),
             pltpu.VMEM((256, pool), BF16),
-            pltpu.VMEM((2, 48, depth), BF16),
+            pltpu.VMEM((2, 96 - KEEP, depth), BF16),
             pltpu.VMEM((2, t, 128), F32),
             pltpu.VMEM((2, 8, 128), F32),
             pltpu.VMEM((t, rows), BF16),

time: 80.5 us -> 80.4 us (level)
  no operation moved by 1% of the time
where the time goes in v4:
time: 80.4 us; the launch traced here: 80.2 us
  Pallas kernels  76.4 us (95%)
  local copies, waits for them, and re-layouts  3.14 us (4%)
    pallas_call x1, Pallas kernels, local(): pl.pallas_call(functools.partial(main_kernel, scale, shift), out_shape=(s...  76.4 us
    unnamed x2, local copies, waits for them, and re-layouts  3.14 us

profile of v4, /device:TPU:1, one launch (start us, length us, event | category | flops | bytes accessed | tf_op | source)
XLA Modules:
  0.0 80.2 jit_solution(9573841609133039186)
XLA Ops:
  0.6 76.4 %shard_map.86 = (f32[16,1024]{1,0:T(8,128)}, f32[16,4096]{1,0:T(8,128)}) custom-call(s32[2,3072]{1,0:T(2,128)} %blk_in.1, bf16[4096,512]{1,0:T(8,128)(2,1)} %centres_in.1, f32[16,4096]{1,0:T(8,128)} %coefs_in.1, bf16[1024,512]{1,0:T(8,128)(2,1)} %samples_in.1, f32[1,1024]{1,0:T(1,128)} %bitcast.1, f32[16,1024]{1,0:T(8,128)} %targets_in.1, f32[16,1024]{1,0:T(8,128)} %preds_in.1), custom_call_target="tpu_custom_call" | custom-call | tf_op jit(solution)/shard_map/pallas_call | solution.py:654
  77.0 1.7 %copy.11 = f32[16,4096]{1,0:T(8,128)} copy(f32[16,4096]{1,0:T(8,128)} %get-tuple-element.8) | data formatting | bytes 524288
  78.7 1.5 %copy.12 = f32[16,1024]{1,0:T(8,128)} copy(f32[16,1024]{1,0:T(8,128)} %get-tuple-element.9) | data formatting | bytes 131072

commit v5 on v4

--- a/solution.py
+++ b/solution.py
@@ -33,7 +33,7 @@
 
 
 def main_kernel(scale, shift, blk_in, centres_in, coefs_in, samples_in, weights_in, targets_in, preds_in,
-                pred_hbm, coef_hbm, pred_out, coef_out,
+                out_hbm, pred_out, coef_out,
                 blk, centres, coefs, samples, weights, targets, preds, select,
                 outgoing, own_coef, place, weighted, samples_t,
                 cent, peer_t, peer_coef, places, wt, peer_wt, auxes, wcat, kt, gsend, grecv, sqsend, sqrecv,
@@ -588,7 +588,7 @@
                 pl.when(core != half)(lambda half=half: e_copy(0, half, 0).start())
     lrecv[e] = lsend[core]
     update_coefs(1, coef_out)
-    store_coef = pltpu.make_async_copy(coef_out, coef_hbm, loads.at[7])
+    store_coef = pltpu.make_async_copy(coef_out, out_hbm.at[:, pl.ds(0, pool)], loads.at[7])
     store_coef.start()
     def drain_last(k, carry):
         f_copy(1, lax.rem(e + k, 8)).wait_send()
@@ -625,7 +625,7 @@
     pred_out[:, 0:512] = pend[0]
     pred_out[:, 512:1024] = pend[1]
 
-    store_pred = pltpu.make_async_copy(pred_out, pred_hbm, loads.at[8])
+    store_pred = pltpu.make_async_copy(pred_out, out_hbm.at[:, pl.ds(pool, pred_out.shape[1])], loads.at[8])
     store_pred.start()
     for rel in range(2):
         for half in range(2):
@@ -651,11 +651,11 @@
     hbm = pl.BlockSpec(memory_space=pl.ANY)
     sds = jax.ShapeDtypeStruct
     dma = pltpu.SemaphoreType.DMA
-    pred, coef = pl.pallas_call(
+    both = pl.pallas_call(
         functools.partial(main_kernel, scale, shift),
-        out_shape=(sds((t, rows), F32), sds((t, pool), F32)),
+        out_shape=sds((t, pool + rows), F32),
         in_specs=[hbm] * 7,
-        out_specs=(hbm,) * 2,
+        out_specs=hbm,
         scratch_shapes=[
             pltpu.VMEM((t, rows), F32),
             pltpu.VMEM((t, pool), F32),
@@ -712,7 +712,7 @@
             collective_id=0, has_side_effects=True, vmem_limit_bytes=60 * 2**20
         ),
     )(block_index, centres, coefs, samples, weights[None, :], targets, predictions)
-    return coef, pred
+    return both[:, :pool], both[:, pool:]
 
 
 def solution(mesh):

time: 80.4 us -> 80.3 us (level)
    slice x0 -> x2, local copies, waits for them, and re-layouts: none -> 3.14 us  [local(): return (both[:, :pool], both[:, pool:])]
    unnamed x2 -> x0, local copies, waits for them, and re-layouts: 3.14 us -> none
where the time goes in v5:
time: 80.3 us; the launch traced here: 80.1 us
  Pallas kernels  76.3 us (95%)
  local copies, waits for them, and re-layouts  3.14 us (4%)
    pallas_call x1, Pallas kernels, local(): pl.pallas_call(functools.partial(main_kernel, scale, shift), out_shape=sd...  76.3 us
    slice x2, local copies, waits for them, and re-layouts, local(): return (both[:, :pool], both[:, pool:])  3.14 us

profile of v5, /device:TPU:1, one launch (start us, length us, event | category | flops | bytes accessed | tf_op | source)
XLA Modules:
  0.0 80.1 jit_solution(11233153949185075763)
XLA Ops:
  0.6 76.3 %shard_map.86 = f32[16,5120]{1,0:T(8,128)} custom-call(s32[2,3072]{1,0:T(2,128)} %blk_in.1, bf16[4096,512]{1,0:T(8,128)(2,1)} %centres_in.1, f32[16,4096]{1,0:T(8,128)} %coefs_in.1, bf16[1024,512]{1,0:T(8,128)(2,1)} %samples_in.1, f32[1,1024]{1,0:T(1,128)} %bitcast.1, f32[16,1024]{1,0:T(8,128)} %targets_in.1, f32[16,1024]{1,0:T(8,128)} %preds_in.1), custom_call_target="tpu_custom_call" | custom-call | tf_op jit(solution)/shard_map/pallas_call | solution.py:654
  76.9 1.5 %slice.7 = f32[16,1024]{1,0:T(8,128)} slice(f32[16,5120]{1,0:T(8,128)} %shard_map.86), slice={[0:16], [4096:5120]} | slice | bytes 131072 | tf_op jit(solution)/shard_map/slice | solution.py:715
  78.4 1.7 %slice.6 = f32[16,4096]{1,0:T(8,128)} slice(f32[16,5120]{1,0:T(8,128)} %shard_map.86), slice={[0:16], [0:4096]} | slice | bytes 524288 | tf_op jit(solution)/shard_map/slice | solution.py:715

commit v6 on v4

--- a/solution.py
+++ b/solution.py
@@ -95,7 +95,7 @@
     lower = (iota((q_rows, q_rows), 0) > iota((q_rows, q_rows), 1)).astype(F32)
     rank_of = iota((128, 128), 0).astype(F32)
     fetch[0].wait()
-    for s in range(2):
+    def extract(s):
         index = jnp.concatenate([blk[s : s + 1, q * 128 : (q + 1) * 128] for q in range(q_rows)], axis=0)
         at = index - r * pool
         mine = jnp.logical_and(at >= 0, at < pool)
@@ -113,13 +113,12 @@
         for k in range(0, pool, 512):
             lanes = (iota((128, 512), 1) + k).astype(F32)
             select[s * 128 : (s + 1) * 128, k : k + 512] = (col == lanes).astype(F32).astype(BF16)
+        rows = jnp.dot(select[s * 128 : (s + 1) * 128, :], centres[...], preferred_element_type=F32).astype(BF16)
+        cent[s, me, 0:KEEP] = rows[0:KEEP]
+        outgoing[s] = rows[KEEP:96]
+
     fetch[1].wait()
-    rows = jnp.dot(select[...], centres[...], preferred_element_type=F32).astype(BF16)
-    for s in range(2):
-        cent[s, me, 0:KEEP] = rows[s * 128 : s * 128 + KEEP]
-        outgoing[s] = rows[s * 128 + KEEP : s * 128 + 96]
-    fetch[2].wait()
-    samples_t[...] = samples[...].T
+    extract(0)
 
     pl.semaphore_wait(barrier, len(neighbours))
 
@@ -203,7 +202,8 @@
 
     half_copy(0).start()
     launch(0, 0)
-    half_copy(1).start()
+    fetch[2].wait()
+    samples_t[...] = samples[...].T
 
     cut = 112
     depth = samples_t.shape[0]
@@ -217,6 +217,8 @@
     ]
     for cp in x_samples:
         cp.start()
+    extract(1)
+    half_copy(1).start()
     hand = [
         remote(peer_t.at[low_f], peer_t.at[low_f], hs.at[0], hr.at[0], sibling),
         remote(peer_t.at[high_f], peer_t.at[high_f], hs.at[1], hr.at[1], sibling),

time: 80.4 us -> 80 us (level)
  no operation moved by 1% of the time
where the time goes in v6:
time: 80 us; the launch traced here: 79.8 us
  Pallas kernels  76 us (95%)
  local copies, waits for them, and re-layouts  3.14 us (4%)
    pallas_call x1, Pallas kernels, local(): pl.pallas_call(functools.partial(main_kernel, scale, shift), out_shape=(s...  76 us
    unnamed x2, local copies, waits for them, and re-layouts  3.14 us

profile of v6, /device:TPU:1, one launch (start us, length us, event | category | flops | bytes accessed | tf_op | source)
XLA Modules:
  0.0 79.8 jit_solution(4700242276665333011)
XLA Ops:
  0.6 76.0 %shard_map.86 = (f32[16,1024]{1,0:T(8,128)}, f32[16,4096]{1,0:T(8,128)}) custom-call(s32[2,3072]{1,0:T(2,128)} %blk_in.1, bf16[4096,512]{1,0:T(8,128)(2,1)} %centres_in.1, f32[16,4096]{1,0:T(8,128)} %coefs_in.1, bf16[1024,512]{1,0:T(8,128)(2,1)} %samples_in.1, f32[1,1024]{1,0:T(1,128)} %bitcast.1, f32[16,1024]{1,0:T(8,128)} %targets_in.1, f32[16,1024]{1,0:T(8,128)} %preds_in.1), custom_call_target="tpu_custom_call" | custom-call | tf_op jit(solution)/shard_map/pallas_call | solution.py:656
  76.6 1.7 %copy.11 = f32[16,4096]{1,0:T(8,128)} copy(f32[16,4096]{1,0:T(8,128)} %get-tuple-element.8) | data formatting | bytes 524288
  78.3 1.5 %copy.12 = f32[16,1024]{1,0:T(8,128)} copy(f32[16,1024]{1,0:T(8,128)} %get-tuple-element.9) | data formatting | bytes 131072
